TPU v7x, 32 devices: a whole 2x2x4 slice. The times are simulated.
32 devices in a mesh: dp: 8 (over z, x), fsdp: 4 (over y, core).
Axes of the slice: x: 2, y: 2, z: 4, core: 2. Of those that a mesh axis runs over, the one named last changes fastest.
Arguments:
- signal: bfloat16 [4, 32768, 512], P('fsdp', 'dp'), may hold values from -6 to 6
- cond: bfloat16 [4, 80, 32768], P('fsdp', None, 'dp'), may hold values from -6 to 6
- clip_lengths: int32 [4, 16], P('fsdp'), may hold values from 1 to 28673, 32768 in all within a row
- dilation: int32 [4], P('fsdp'), may hold values from 1 to 512, as said below
- w_conv: bfloat16 [2, 512, 1024], P(None, ('dp', 'fsdp')), may hold values from -0.1875 to 0.1875
- w_cond: bfloat16 [80, 1024], P(None, ('dp', 'fsdp')), may hold values from -0.625 to 0.625
- b_conv: bfloat16 [1024], P(('dp', 'fsdp')), may hold values from -3 to 3
- w_res: bfloat16 [512, 512], P(('dp', 'fsdp')), may hold values from -0.5 to 0.5
- b_res: bfloat16 [512], P(('dp', 'fsdp')), may hold values from -3 to 3
- w_skip: bfloat16 [512, 512], P(('dp', 'fsdp')), may hold values from -0.5 to 0.5
- b_skip: bfloat16 [512], P(('dp', 'fsdp')), may hold values from -3 to 3
- cot_res: bfloat16 [4, 32768, 512], P('fsdp', 'dp'), may hold values from -6 to 6
- cot_skip: bfloat16 [4, 32768, 512], P('fsdp', 'dp'), may hold values from -6 to 6
Outputs:
- res_out: bfloat16 [4, 32768, 512], P('fsdp', 'dp')
- skip_out: bfloat16 [4, 32768, 512], P('fsdp', 'dp')
- grad_signal: float32 [4, 32768, 512], P('fsdp', 'dp')
- grad_w_conv: float32 [2, 512, 1024], P(None, ('dp', 'fsdp'))
- grad_w_cond: float32 [80, 1024], P(None, ('dp', 'fsdp'))
- grad_b_conv: float32 [1024], P(('dp', 'fsdp'))
- grad_w_res: float32 [512, 512], P(('dp', 'fsdp'))
- grad_b_res: float32 [512], P(('dp', 'fsdp'))
- grad_w_skip: float32 [512, 512], P(('dp', 'fsdp'))
- grad_b_skip: float32 [512], P(('dp', 'fsdp'))
Inputs may be any that keep to these rules, and one draw needn't show every extreme that they name: `clip_lengths`: each row sums to 32768; in each stream one clip is exactly 28673 samples long. Some stream has dilation exactly 512.
All inputs are finite; a program needn't handle non-finite values.
Results may differ from a plain program's by a relative error of at most 0.0044.
Values may be sent and summed in bfloat16 or wider, within the bound.
A program may use at most 128 MiB of HBM per device.

v0:
```python
import jax
import jax.numpy as jnp
from jax import lax
from jax.sharding import PartitionSpec as P

DMAX = 512


def from_behind(value, axis, steps):
    count = lax.axis_size(axis)
    first, last = (max(0, -steps), min(count, count - steps))
    return lax.ppermute(value, axis, [(source, source + steps) for source in range(first, last)])


def matmul(left, right):
    return jnp.dot(left, right, preferred_element_type=jnp.float32)


def contract_first(left, right):
    return lax.dot_general(
        left, right, (((0,), (0,)), ((), ())), preferred_element_type=jnp.float32
    )


def contract_last(left, right):
    return lax.dot_general(
        left, right, (((1,), (1,)), ((), ())), preferred_element_type=jnp.float32
    )


def shards(
    signal,
    cond,
    clip_lengths,
    dilation,
    w_conv,
    w_cond,
    b_conv,
    w_res,
    b_res,
    w_skip,
    b_skip,
    cot_res,
    cot_skip,
):
    rows = signal.shape[1]
    chans = signal.shape[2]
    conv_full, cond_full, bconv_full, res_full, bres_full, skip_full, bskip_full = (
        lax.all_gather(w_conv, ("dp", "fsdp"), axis=1, tiled=True),
        lax.all_gather(w_cond, ("dp", "fsdp"), axis=1, tiled=True),
        lax.all_gather(b_conv, ("dp", "fsdp"), axis=0, tiled=True),
        lax.all_gather(w_res, ("dp", "fsdp"), axis=0, tiled=True),
        lax.all_gather(b_res, ("dp", "fsdp"), axis=0, tiled=True),
        lax.all_gather(w_skip, ("dp", "fsdp"), axis=0, tiled=True),
        lax.all_gather(b_skip, ("dp", "fsdp"), axis=0, tiled=True),
    )
    segment = lax.axis_index("dp")
    times = segment * rows + jnp.arange(rows, dtype=jnp.int32)
    lengths = clip_lengths[0]
    starts = jnp.cumsum(lengths) - lengths
    begin = jnp.max(jnp.where(starts[None, :] <= times[:, None], starts[None, :], 0), axis=1)
    dilate = dilation[0]
    keep = times - begin >= dilate
    mask_low = keep.astype(jnp.bfloat16)
    samples = signal[0]
    conds = cond[0]
    tail = from_behind(samples[rows - DMAX :], "dp", 1)
    extended = jnp.concatenate([tail, samples], 0)
    lagged = lax.dynamic_slice_in_dim(extended, DMAX - dilate, rows, 0) * mask_low[:, None]
    preact = (
        matmul(lagged, conv_full[0])
        + matmul(samples, conv_full[1])
        + contract_first(conds, cond_full)
        + bconv_full.astype(jnp.float32)
    )
    half = preact.shape[1] // 2
    tanh_part = jnp.tanh(preact[:, :half])
    sig_part = jax.nn.sigmoid(preact[:, half:])
    gated = (tanh_part * sig_part).astype(jnp.bfloat16)
    res_out = (
        samples.astype(jnp.float32) + matmul(gated, res_full) + bres_full.astype(jnp.float32)
    ).astype(jnp.bfloat16)
    skip_out = (matmul(gated, skip_full) + bskip_full.astype(jnp.float32)).astype(jnp.bfloat16)
    conv_back, cond_back, bconv_back, res_back, bres_back, skip_back, bskip_back = (
        lax.all_gather(w_conv, ("dp", "fsdp"), axis=1, tiled=True),
        lax.all_gather(w_cond, ("dp", "fsdp"), axis=1, tiled=True),
        lax.all_gather(b_conv, ("dp", "fsdp"), axis=0, tiled=True),
        lax.all_gather(w_res, ("dp", "fsdp"), axis=0, tiled=True),
        lax.all_gather(b_res, ("dp", "fsdp"), axis=0, tiled=True),
        lax.all_gather(w_skip, ("dp", "fsdp"), axis=0, tiled=True),
        lax.all_gather(b_skip, ("dp", "fsdp"), axis=0, tiled=True),
    )
    back_res = cot_res[0]
    back_skip = cot_skip[0]
    d_gated = contract_last(back_res, res_back) + contract_last(back_skip, skip_back)
    d_preact = jnp.concatenate(
        [
            d_gated * sig_part * (1.0 - tanh_part * tanh_part),
            d_gated * tanh_part * sig_part * (1.0 - sig_part),
        ],
        1,
    ).astype(jnp.bfloat16)
    grad_res = contract_first(gated, back_res)
    grad_bres = jnp.sum(back_res.astype(jnp.float32), axis=0)
    grad_skip = contract_first(gated, back_skip)
    grad_bskip = jnp.sum(back_skip.astype(jnp.float32), axis=0)
    grad_conv = jnp.stack([contract_first(lagged, d_preact), contract_first(samples, d_preact)])
    grad_cond = matmul(conds, d_preact)
    grad_bconv = jnp.sum(d_preact.astype(jnp.float32), axis=0)
    grad_in = back_res.astype(jnp.float32) + contract_last(d_preact, conv_back[1])
    d_lagged = contract_last(d_preact, conv_back[0]) * keep.astype(jnp.float32)[:, None]
    d_extended = jnp.zeros((DMAX + rows, chans), jnp.float32)
    d_extended = lax.dynamic_update_slice_in_dim(d_extended, d_lagged, DMAX - dilate, 0)
    grad_in = grad_in + d_extended[DMAX:]
    returned = from_behind(d_extended[:DMAX].astype(jnp.bfloat16), "dp", -1).astype(jnp.float32)
    grad_in = grad_in + jnp.concatenate([jnp.zeros((rows - DMAX, chans), jnp.float32), returned], 0)
    sums = (
        lax.psum_scatter(grad_conv, ("dp", "fsdp"), scatter_dimension=1, tiled=True),
        lax.psum_scatter(grad_cond, ("dp", "fsdp"), scatter_dimension=1, tiled=True),
        lax.psum_scatter(grad_bconv, ("dp", "fsdp"), scatter_dimension=0, tiled=True),
        lax.psum_scatter(grad_res, ("dp", "fsdp"), scatter_dimension=0, tiled=True),
        lax.psum_scatter(grad_bres, ("dp", "fsdp"), scatter_dimension=0, tiled=True),
        lax.psum_scatter(grad_skip, ("dp", "fsdp"), scatter_dimension=0, tiled=True),
        lax.psum_scatter(grad_bskip, ("dp", "fsdp"), scatter_dimension=0, tiled=True),
    )
    return (
        res_out[None],
        skip_out[None],
        grad_in[None],
        sums[0],
        sums[1],
        sums[2],
        sums[3],
        sums[4],
        sums[5],
        sums[6],
    )


def solution(mesh):
    return jax.shard_map(
        shards,
        mesh=mesh,
        in_specs=(
            P("fsdp", "dp", None),
            P("fsdp", None, "dp"),
            P("fsdp", None),
            P("fsdp"),
            P(None, ("dp", "fsdp"), None),
            P(None, ("dp", "fsdp")),
            P(("dp", "fsdp")),
            P(("dp", "fsdp"), None),
            P(("dp", "fsdp")),
            P(("dp", "fsdp"), None),
            P(("dp", "fsdp")),
            P("fsdp", "dp", None),
            P("fsdp", "dp", None),
        ),
        out_specs=(
            P("fsdp", "dp", None),
            P("fsdp", "dp", None),
            P("fsdp", "dp", None),
            P(None, ("dp", "fsdp"), None),
            P(None, ("dp", "fsdp")),
            P(("dp", "fsdp")),
            P(("dp", "fsdp"), None),
            P(("dp", "fsdp")),
            P(("dp", "fsdp"), None),
            P(("dp", "fsdp")),
        ),
        check_vma=False,
    )
```

profile of v0, /device:TPU:0, one launch (start us, length us, event | category | flops | bytes accessed | tf_op | source)
XLA Modules:
  0.0 800.4 jit_solution(4414945298574294403)
XLA Ops:
  9.1 5.7 collective-permute-start
  17.2 44.3 %all-reduce.8 = (bf16[1024]{0:T(1024)(128)(2,1)S(1)}, bf16[512]{0:T(512)(128)(2,1)S(1)}, bf16[512]{0:T(512)(128)(2,1)S(1)}) all-reduce(bf16[1024]{0:T(1024)(128)(2,1)S(1)} %dynamic-update-slice, bf16[512]{0:T(512)(128)(2,1)S(1)} %dynamic-update-slice.1, ...), channel_id=1, replica_groups=mesh['dp'=8,'fsdp'=4] {'dp','fsdp'}, use_global_device_ids=true, to_apply=%add.1 | all-reduce | flops 2048 | bytes 8192
  63.9 40.5 %all_gather.25 = bf16[80,1024]{0,1:T(8,128)(2,1)S(1)} all-gather(bf16[80,32]{0,1:T(8,128)(2,1)} %param.18), channel_id=1, replica_groups=mesh['dp'=8,'fsdp'=4] {'dp','fsdp'}, dimensions={1}, use_global_device_ids=true | all-gather | bytes 168960 | tf_op jit(solution)/shard_map/all_gather | solution.py:50
  104.4 38.3 %all_gather.27 = bf16[512,512]{1,0:T(8,128)(2,1)S(1)} all-gather(bf16[16,512]{1,0:T(8,128)(2,1)} %param.20), channel_id=1, replica_groups=mesh['dp'=8,'fsdp'=4] {'dp','fsdp'}, dimensions={0}, use_global_device_ids=true | all-gather | bytes 540672 | tf_op jit(solution)/shard_map/all_gather | solution.py:52
  142.7 42.3 %all_gather.29 = bf16[512,512]{1,0:T(8,128)(2,1)} all-gather(bf16[16,512]{1,0:T(8,128)(2,1)} %param.22), channel_id=1, replica_groups=mesh['dp'=8,'fsdp'=4] {'dp','fsdp'}, dimensions={0}, use_global_device_ids=true | all-gather | bytes 540672 | tf_op jit(solution)/shard_map/all_gather | solution.py:54
  185.0 8.0 %fusion.15 = f32[4096,512]{0,1:T(8,128)} fusion(bf16[512,512]{1,0:T(8,128)(2,1)S(1)} %all_gather.27, bf16[1,4096,512]{2,1,0:T(8,128)(2,1)} %param.24), kind=kOutput, calls=%fused_computation.33 | convolution fusion | flops 2147483648 | bytes 13107200 | tf_op jit(solution)/shard_map/dot_general | solution.py:26
  193.0 8.0 %fusion.20 = f32[4096,1024]{0,1:T(8,128)} fusion(bf16[80,1024]{0,1:T(8,128)(2,1)S(1)} %all_gather.25, bf16[1,80,4096]{2,1,0:T(8,128)(2,1)S(1)} %copy-done), kind=kOutput, calls=%fused_computation.44 | convolution fusion | flops 671088640 | bytes 17596416 | tf_op jit(solution)/shard_map/dot_general | solution.py:20
  201.0 12.9 %fusion.18 = f32[4096,1024]{0,1:T(8,128)} fusion(bf16[2,512,1024]{2,1,0:T(8,128)(2,1)} %all-gather.2.cloned.1.call-done, bf16[1,4096,512]{2,1,0:T(8,128)(2,1)} %param.13), kind=kOutput, calls=%fused_computation.42 | convolution fusion | flops 4294967296 | bytes 22020096 | tf_op jit(solution)/shard_map/dot_general | solution.py:16
  214.0 21.9 %add_add_fusion = f32[4096,1024]{0,1:T(8,128)} fusion(f32[4096,1024]{0,1:T(8,128)} %fusion.20, f32[4096,1024]{0,1:T(8,128)} %fusion.18, f32[1024]{0:T(1024)S(1)} %convert_element_type.50, bf16[2,512,1024]{2,1,0:T(8,128)(2,1)} %all-gather.2.cloned.1.call-done, s32[]{:T(128)S(6)} %select_n.8, bf16[512,512]{1,0:T(8,128)(2,1)} %collective-permute-done, ...), kind=kOutput, calls=%fused_computation.1 | convolution fusion | flops 4320133120 | bytes 56111108 | tf_op jit(solution)/shard_map/dot_general | solution.py:16
  235.9 14.1 %multiply_convert_fusion.1 = (bf16[4096,512]{0,1:T(8,128)(2,1)}, bf16[4096,512]{0,1:T(8,128)(2,1)}, bf16[4096,512]{0,1:T(8,128)(2,1)}) fusion(f32[4096,1024]{0,1:T(8,128)} %add_add_fusion, f32[4096,512]{0,1:T(8,128)S(1)} %bitcast.70, bf16[512,512]{1,0:T(8,128)(2,1)} %all_gather.29, bf16[1,4096,512]{2,1,0:T(8,128)(2,1)} %param.25), kind=kOutput, calls=%fused_computation.15 | convolution fusion | flops 2181038080 | bytes 42467328 | tf_op jit(solution)/shard_map/dot_general | solution.py:26
  250.0 5.0 convolution_bitcast_fusion.2
  256.1 6.8 fusion.10
  263.0 6.8 fusion.13
  270.1 10.4 %convolution_bitcast_fusion.1 = f32[1,512,1024]{2,1,0:T(8,128)S(1)} fusion(s32[]{:T(128)S(6)} %select_n.8, bf16[512,512]{1,0:T(8,128)(2,1)} %collective-permute-done, bf16[4096,512]{1,0:T(8,128)(2,1)} %bitcast.72, bf16[4096]{0:T(1024)(128)(2,1)S(1)} %convert_element_type.49, bf16[4096,512]{0,1:T(8,128)(2,1)} %get-tuple-element.49, ...), kind=kOutput, calls=%fused_computation.36 | convolution fusion | flops 4324327424 | bytes 15212548 | tf_op jit(solution)/shard_map/dot_general | solution.py:20
  280.6 8.1 %convolution_bitcast_fusion = f32[1,512,1024]{2,1,0:T(8,128)} fusion(bf16[1,4096,512]{2,1,0:T(8,128)(2,1)S(1)} %copy-done.3, bf16[4096,512]{0,1:T(8,128)(2,1)} %get-tuple-element.49, bf16[4096,512]{0,1:T(8,128)(2,1)S(1)} %copy-done.4), kind=kOutput, calls=%fused_computation.35 | convolution fusion | flops 4311744512 | bytes 14680064 | tf_op jit(solution)/shard_map/dot_general | solution.py:20
  299.3 8.2 %convolution_multiply_fusion = f32[4096,512]{1,0:T(8,128)} fusion(f32[4096]{0:T(1024)S(1)} %get-tuple-element.46, bf16[2,512,1024]{2,1,0:T(8,128)(2,1)} %all-gather.2.cloned.1.call-done, bf16[4096,512]{0,1:T(8,128)(2,1)S(1)} %copy-done.7, bf16[4096,512]{0,1:T(8,128)(2,1)S(1)} %copy-done.5), kind=kOutput, calls=%fused_computation.20 | convolution fusion | flops 4313841664 | bytes 17842176 | tf_op jit(solution)/shard_map/dot_general | solution.py:26
  307.5 4.8 broadcast_in_dim.34
  312.4 22.1 %dynamic_update_slice.3 = f32[4608,512]{1,0:T(8,128)} dynamic-update-slice(f32[4608,512]{1,0:T(8,128)} %broadcast_in_dim.34, f32[4096,512]{1,0:T(8,128)} %convolution_multiply_fusion, s32[]{:T(128)S(6)} %select_n.8, s32[]{:T(128)} %constant.11.clone.1) | dynamic-update-slice | bytes 16777220 | tf_op jit(solution)/shard_map/dynamic_update_slice | solution.py:113
  342.5 41.8 %all-reduce.7 = (f32[1024]{0:T(1024)S(1)}, f32[512]{0:T(512)S(1)}, f32[512]{0:T(512)S(1)}) all-reduce(f32[1024]{0:T(1024)S(1)} %convert_reduce_fusion, f32[512]{0:T(512)S(1)} %convert_reduce_fusion.1, f32[512]{0:T(512)S(1)} %convert_reduce_fusion.2), channel_id=4, replica_groups=mesh['dp'=8,'fsdp'=4] {'dp','fsdp'}, use_global_device_ids=true, to_apply=%region_5.6.clone | all-reduce | flops 2048 | bytes 16384
  386.0 8.3 %fusion.7 = bf16[1,4096,512]{2,1,0:T(8,128)(2,1)} fusion(bf16[4096,512]{0,1:T(8,128)(2,1)} %get-tuple-element.50, bf16[512,512]{1,0:T(8,128)(2,1)S(1)} %all_gather.27, f32[512]{0:T(512)S(1)} %convert_element_type.52, bf16[1,4096,512]{2,1,0:T(8,128)(2,1)} %param.13), kind=kOutput, calls=%fused_computation.22 | convolution fusion | flops 2155872256 | bytes 13109248 | tf_op jit(solution)/shard_map/dot_general | solution.py:16
  399.8 11.3 %fusion.2 = f32[1,4096,512]{2,1,0:T(8,128)} fusion(f32[4608,512]{1,0:T(8,128)} %dynamic_update_slice.3, bf16[1,4096,512]{2,1,0:T(8,128)(2,1)S(1)} %copy-done.2, bf16[512,512]{1,0:T(8,128)(2,1)} %collective-permute-done.1, bf16[2,512,1024]{2,1,0:T(8,128)(2,1)S(1)} %copy-done.8, bf16[4096,512]{0,1:T(8,128)(2,1)} %get-tuple-element.49, ...), kind=kOutput, calls=%fused_computation.6 | convolution fusion | flops 4322230272 | bytes 30932992 | tf_op jit(solution)/shard_map/dot_general | solution.py:26
  411.1 109.0 %reduce-scatter.11.cloned.1.call-done = f32[16,512]{1,0:T(8,128)} async-done(((f32[512,512]{1,0:T(8,128)}), f32[16,512]{1,0:T(8,128)}) %reduce-scatter.11.cloned.1.call-update) | async-done | bytes 32784 | tf_op jit(solution)/shard_map/reduce_scatter | solution.py:123
  520.1 133.4 %reduce-scatter.9.cloned.1.call-done = f32[16,512]{1,0:T(8,128)} async-done(((f32[512,512]{1,0:T(8,128)}), f32[16,512]{1,0:T(8,128)}) %reduce-scatter.9.cloned.1.call-update) | async-done | bytes 32784 | tf_op jit(solution)/shard_map/reduce_scatter | solution.py:121
  653.4 140.0 %reduce-scatter.7.cloned.1.call-done = f32[2,16,1024]{2,1,0:T(8,128)} async-done(((f32[2,512,1024]{2,1,0:T(8,128)}), f32[2,16,1024]{2,1,0:T(8,128)}) %reduce-scatter.7.cloned.1.call-update) | async-done | bytes 131088 | tf_op jit(solution)/shard_map/reduce_scatter | solution.py:118
  (68 shorter events, 33.3 us)
Async XLA Ops:
  7.2 185.8 %copy-start = (bf16[1,80,4096]{2,1,0:T(8,128)(2,1)S(1)}, bf16[1,80,4096]{2,1,0:T(8,128)(2,1)}, u32[]{:S(2)}) copy-start(bf16[1,80,4096]{2,1,0:T(8,128)(2,1)} %param.14) | copy-start | bytes 1966084
  7.2 193.8 %all-gather.2.cloned.1.call-start = ((), (), s32[]{:S(2)}) async-start(), calls=%async_computation.4 | async-start | bytes 2162688 | tf_op jit(solution)/shard_map/all_gather | solution.py:49
  7.9 403.2 %reduce-scatter.13.cloned.1.call-start = ((), (), s32[]{:S(2)}) async-start(), calls=%async_computation.8 | async-start | bytes 540672
  9.1 204.9 %collective-permute-start = (bf16[512,512]{1,0:T(8,128)(2,1)S(1)}, bf16[512,512]{1,0:T(8,128)(2,1)}, u32[]{:S(2)}, u32[]{:S(2)}) collective-permute-start(bf16[512,512]{1,0:T(8,128)(2,1)S(1)} %slice_bitcast_fusion.8), channel_id=1, source_target_pairs={{0,4},{4,8},{8,12},{12,16},{16,20},{20,24},{24,28},{1,5},{5,9},{9,... | collective-permute-start | bytes 1572872 | tf_op jit(solution)/shard_map/ppermute | solution.py:12
  201.0 34.8 %slice-start = ((s8[8388608]{0:T(1024)(128)(4,1)}), s8[4194304]{0:T(1024)(128)(4,1)S(1)}, s32[]{:S(2)}) async-start(s8[8388608]{0:T(1024)(128)(4,1)} %bitcast.69), calls=%async_computation.9 | async-start | bytes 8388608
  214.0 21.9 %slice-start.1 = ((s8[8388608]{0:T(1024)(128)(4,1)}), s8[4194304]{0:T(1024)(128)(4,1)S(1)}, s32[]{:S(2)}) async-start(s8[8388608]{0:T(1024)(128)(4,1)} %bitcast.69), calls=%async_computation.10 | async-start | bytes 8388608
  256.0 264.0 %reduce-scatter.11.cloned.1.call-start = ((), (), s32[]{:S(2)}) async-start(), calls=%async_computation.7 | async-start | bytes 1081344 | tf_op jit(solution)/shard_map/reduce_scatter | solution.py:123
  262.9 390.5 %reduce-scatter.9.cloned.1.call-start = ((), (), s32[]{:S(2)}) async-start(), calls=%async_computation.6 | async-start | bytes 1081344 | tf_op jit(solution)/shard_map/reduce_scatter | solution.py:121
  269.8 523.6 %reduce-scatter.7.cloned.1.call-start = ((), (), s32[]{:S(2)}) async-start(), calls=%async_computation.5 | async-start | bytes 4325376 | tf_op jit(solution)/shard_map/reduce_scatter | solution.py:118
  270.1 10.5 %copy-start.3 = (bf16[1,4096,512]{2,1,0:T(8,128)(2,1)S(1)}, bf16[1,4096,512]{2,1,0:T(8,128)(2,1)}, u32[]{:S(2)}) copy-start(bf16[1,4096,512]{2,1,0:T(8,128)(2,1)} %param.13) | copy-start | bytes 12582916
  270.1 10.5 %copy-start.4 = (bf16[4096,512]{0,1:T(8,128)(2,1)S(1)}, bf16[4096,512]{0,1:T(8,128)(2,1)}, u32[]{:S(2)}) copy-start(bf16[4096,512]{0,1:T(8,128)(2,1)} %get-tuple-element.48) | copy-start | bytes 12582916
  292.8 6.5 copy-start.5
  292.8 6.5 copy-start.7
  336.6 62.3 %collective-permute-start.1 = (bf16[512,512]{1,0:T(8,128)(2,1)}, bf16[512,512]{1,0:T(8,128)(2,1)}, u32[]{:S(2)}, u32[]{:S(2)}) collective-permute-start(bf16[512,512]{1,0:T(8,128)(2,1)} %slice.72), channel_id=1, source_target_pairs={{4,0},{8,4},{12,8},{16,12},{20,16},{24,20},{28,24},{5,1},{9,5},{13... | collective-permute-start | bytes 1572872 | tf_op jit(solution)/shard_map/ppermute | solution.py:12
  386.0 8.3 %copy-start.9 = (bf16[512,512]{1,0:T(8,128)(2,1)S(1)}, bf16[512,512]{1,0:T(8,128)(2,1)}, u32[]{:S(2)}) copy-start(bf16[512,512]{1,0:T(8,128)(2,1)} %all_gather.29) | copy-start | bytes 1572868
  386.0 8.3 %copy-start.10 = (bf16[4096,512]{0,1:T(8,128)(2,1)S(1)}, bf16[4096,512]{0,1:T(8,128)(2,1)}, u32[]{:S(2)}) copy-start(bf16[4096,512]{0,1:T(8,128)(2,1)} %get-tuple-element.50) | copy-start | bytes 12582916
  394.4 4.6 copy-start.2
  394.4 4.6 copy-start.6
  394.4 5.4 copy-start.8
  399.8 393.7 %copy-start.1 = (bf16[1,80,4096]{2,1,0:T(8,128)(2,1)S(1)}, bf16[1,80,4096]{2,1,0:T(8,128)(2,1)}, u32[]{:S(2)}) copy-start(bf16[1,80,4096]{2,1,0:T(8,128)(2,1)} %param.14) | copy-start | bytes 1966084
Sparse Core Ops, SparseCore 0:
  10.9 61.3 all-gather.1
  256.2 130.2 reduce-scatter.12
  389.3 130.7 reduce-scatter.10
  522.7 130.6 reduce-scatter.8
  656.2 137.1 reduce-scatter.6
where the time goes:
time: 810 us; the launch traced here: 800 us
  waiting for transfers between devices  383 us (47%)
  blocking collectives  207 us (26%)
  matrix products  134 us (17%)
  local copies, waits for them, and re-layouts  36.3 us (4%)
  other arithmetic  17 us (2%)
  between operations  15.1 us (2%)
    reduce_scatter x1, waiting for transfers between devices, shards(): lax.psum_scatter(grad_conv, ('dp', 'fsdp'), scatter_dimension=1, tiled=True)  140 us
    reduce_scatter x1, waiting for transfers between devices, shards(): lax.psum_scatter(grad_res, ('dp', 'fsdp'), scatter_dimension=0, tiled=True)  133 us
    reduce_scatter x1, waiting for transfers between devices, shards(): lax.psum_scatter(grad_skip, ('dp', 'fsdp'), scatter_dimension=0, tiled=True)  109 us
    unnamed x2, blocking collectives  86.1 us
    dot_general x5, matrix products, matmul(): return jnp.dot(left, right, preferred_element_type=jnp.float32)  52.7 us
    all_gather x1, blocking collectives, shards(): lax.all_gather(w_skip, ('dp', 'fsdp'), axis=0, tiled=True)  42.3 us
    dot_general x4, matrix products, contract_last(): lax.dot_general(left, right, (((1,), (1,)), ((), ())), preferred_element_...  41.6 us
    all_gather x1, blocking collectives, shards(): lax.all_gather(w_cond, ('dp', 'fsdp'), axis=1, tiled=True)  40.5 us
  transfers between devices with their start and end apart: 7, of which 3 were waited for; matrix products, arithmetic and copies ran while one was open for 18% of the time, Pallas kernels for 0%

commit v1 on v0

--- a/solution.py
+++ b/solution.py
@@ -1,9 +1,607 @@
+import functools
+
 import jax
 import jax.numpy as jnp
 from jax import lax
+from jax.experimental import pallas as pl
+from jax.experimental.pallas import tpu as pltpu
 from jax.sharding import PartitionSpec as P
 
 DMAX = 512
+TILE = 512
+MESH = pl.DeviceIdType.MESH
+BF16 = jnp.bfloat16
+F32 = jnp.float32
+
+
+def matmul(left, right):
+    return jnp.dot(left, right, preferred_element_type=F32)
+
+
+def contract_first(left, right):
+    return lax.dot_general(left, right, (((0,), (0,)), ((), ())), preferred_element_type=F32)
+
+
+def contract_last(left, right):
+    return lax.dot_general(left, right, (((1,), (1,)), ((), ())), preferred_element_type=F32)
+
+
+def bias_places(skip):
+    n = lax.broadcasted_iota(jnp.int32, (512, 1024), 0)
+    m = lax.broadcasted_iota(jnp.int32, (512, 1024), 1)
+    place = (n // 16) * 32 + n % 16 + 16 * skip
+    return jnp.where(place == m, 1.0, 0.0).astype(BF16)
+
+
+def layer_kernel(
+    clip_ref, dil_ref, wconv_ref, wres_ref, wskip_ref, wb_ref, sig_hbm, cond_hbm, cr_hbm, cs_hbm,
+    gated_hbm, e_hbm, wrs_hbm, bias_ref, gconv_ref, gres_ref, gskip_ref, gcond_ref,
+    X, D, condv, W, WC, wct, F, halo, ret_send, ret_recv,
+    Gt, GA, CS, CR, S1, R1, S2, R2, S3, R3,
+    cGA, cCS, cCR, cS1, cR1, cS2, cR2, cS3, cR3,
+    ld, st_g, st_e, st_w, ag_s, ag_r, h_s, h_r, rs_s, rs_r,
+):
+    T = sig_hbm.shape[0]
+    tiles = T // TILE
+    dp, fs = lax.axis_index("dp"), lax.axis_index("fsdp")
+    z, x, y, c = dp // 2, dp % 2, fs // 2, fs % 2
+    x1, y1, c1 = 1 - x, 1 - y, 1 - c
+    zs = (z + 1 - 2 * (z % 2), (z + 2) % 4, 3 - z)
+
+    def dev(zz, xx, yy, cc):
+        return (zz * 2 + xx, yy * 2 + cc)
+
+    sib, xn, yn = dev(z, x, y, c1), dev(z, x1, y, c), dev(z, x, y1, c)
+    zn = [dev(zz, x, y, c) for zz in zs]
+
+    def rcopy(src, dst, ssem, rsem, to):
+        return pltpu.make_async_remote_copy(
+            src_ref=src, dst_ref=dst, send_sem=ssem, recv_sem=rsem, device_id=to, device_id_type=MESH
+        )
+
+    loads = [
+        pltpu.make_async_copy(sig_hbm, X.at[1], ld.at[0]),
+        pltpu.make_async_copy(cr_hbm, D.at[0], ld.at[1]),
+        pltpu.make_async_copy(cs_hbm, D.at[1], ld.at[2]),
+        pltpu.make_async_copy(cond_hbm, condv.at[pl.ds(0, 80)], ld.at[3]),
+    ]
+    for load in loads:
+        load.start()
+
+    extra = dp - 1 + 2 * x
+    has_extra = (extra >= 0) & (extra < 8)
+    barrier = pltpu.get_barrier_semaphore()
+    for to in [sib, xn, yn] + zn:
+        pl.semaphore_signal(barrier, inc=1, device_id=to, device_id_type=MESH)
+
+    @pl.when(has_extra)
+    def _():
+        pl.semaphore_signal(barrier, inc=1, device_id=(extra, fs), device_id_type=MESH)
+        pl.semaphore_wait(barrier, 7)
+
+    @pl.when(jnp.logical_not(has_extra))
+    def _():
+        pl.semaphore_wait(barrier, 6)
+
+    W[0, z, x, y, c] = wconv_ref[0]
+    W[1, z, x, y, c] = wconv_ref[1]
+    W[2, z, x, y, c, :, 0:512] = wres_ref[...]
+    W[2, z, x, y, c, :, 512:1024] = wskip_ref[...]
+    WC[z, x, y, c] = wb_ref[...]
+    sections = (2, 1, 0, 3)
+
+    def along_z(s):
+        own = W.at[s, z, x, y, c] if s < 3 else WC.at[z, x, y, c]
+        return [rcopy(own, own, ag_s.at[s, k], ag_r.at[s, k], zn[k]) for k in range(3)]
+
+    def along_one(s):
+        if s < 3:
+            a, b = W.at[s, :, x, y, c, :, pl.ds(0, 512)], W.at[s, :, x, y, c, :, pl.ds(512, 512)]
+            return [
+                rcopy(a, a, ag_s.at[s, 3], ag_r.at[s, 3], xn),
+                rcopy(b, b, ag_s.at[s, 4], ag_r.at[s, 4], yn),
+            ]
+        a = WC.at[:, x, y, c]
+        return [rcopy(a, a, ag_s.at[s, 3], ag_r.at[s, 3], xn)]
+
+    def along_other(s):
+        if s < 3:
+            a, b = W.at[s, :, :, y, c, :, pl.ds(0, 512)], W.at[s, :, x, :, c, :, pl.ds(512, 512)]
+            return [
+                rcopy(a, a, ag_s.at[s, 5], ag_r.at[s, 5], yn),
+                rcopy(b, b, ag_s.at[s, 6], ag_r.at[s, 6], xn),
+            ]
+        a = WC.at[:, :, y, c]
+        return [rcopy(a, a, ag_s.at[s, 5], ag_r.at[s, 5], yn)]
+
+    def along_core(s):
+        a = W.at[s, :, :, :, c] if s < 3 else WC.at[:, :, :, c]
+        return [rcopy(a, a, ag_s.at[s, 7], ag_r.at[s, 7], sib)]
+
+    def start(copies):
+        for copy in copies:
+            copy.start()
+
+    def wait(copies):
+        for copy in copies:
+            copy.wait()
+
+    for s in sections:
+        start(along_z(s))
+
+    dilate = dil_ref[0]
+    lane = lax.broadcasted_iota(jnp.int32, (1, 128), 1)
+    starts = jnp.zeros((1, 128), jnp.int32)
+    for i in range(16):
+        starts = starts + jnp.where(lane > i, clip_ref[0, i], 0)
+    row = lax.broadcasted_iota(jnp.int32, (TILE, 128), 0)
+
+    def keep(i):
+        times = dp * T + i * TILE + row
+        inside = (starts <= times) & (starts > times - dilate)
+        return 1.0 - jnp.max(jnp.where(inside, 1.0, 0.0), axis=1, keepdims=True)
+
+    def at(i):
+        return pl.ds(pl.multiple_of(i * TILE, TILE), TILE)
+
+    def put(half, value):
+        for n in range(4):
+            F[n, half * TILE : half * TILE + TILE] = value[:, n * 128 : n * 128 + 128].astype(F32)
+
+    def shifted(first):
+        return jnp.concatenate([F[n, pl.ds(first, TILE), :] for n in range(4)], 1)
+
+    def lag_tile(i):
+        put(1, X[1, at(i)])
+        X[2, at(i)] = (shifted(TILE - dilate) * keep(i)).astype(BF16)
+
+    loads[0].wait()
+
+    def lag_body(i, carry):
+        put(0, X[1, at(i - 1)])
+        lag_tile(i)
+        return carry
+
+    lax.fori_loop(1, 3, lag_body, 0)
+    for s in sections:
+        wait(along_z(s))
+        start(along_one(s))
+    lax.fori_loop(3, 6, lag_body, 0)
+    for s in sections:
+        wait(along_one(s))
+        start(along_other(s))
+
+    halo_copy = rcopy(X.at[1, pl.ds(T - DMAX, DMAX)], halo, h_s.at[0], h_r.at[0], (dp + 1, fs))
+
+    @pl.when(dp < 7)
+    def _():
+        halo_copy.start()
+
+    @pl.when(dp == 0)
+    def _():
+        halo[...] = jnp.zeros_like(halo)
+
+    @pl.when(dp == 7)
+    def _():
+        ret_recv[...] = jnp.zeros_like(ret_recv)
+
+    lax.fori_loop(6, tiles, lag_body, 0)
+    condv[80:96] = jnp.where(lax.broadcasted_iota(jnp.int32, (16, T), 0) == 0, 1.0, 0.0).astype(BF16)
+    condv[96:128] = jnp.zeros((32, T), BF16)
+    for load in loads[1:]:
+        load.wait()
+    for s in sections:
+        wait(along_other(s))
+        start(along_core(s))
+
+    wait(along_core(2))
+    wrs_copy = pltpu.make_async_copy(W.at[2], wrs_hbm, st_w.at[0])
+    wrs_copy.start()
+    wrs = W[2].reshape(512, 1024)
+    wres, wskip = wrs[:, :512], wrs[:, 512:]
+
+    def dg_body(i, carry):
+        dg = contract_last(D[0, at(i)], wres) + contract_last(D[1, at(i)], wskip)
+        high = dg.astype(BF16)
+        D[2, at(i)] = high
+        D[3, at(i)] = (dg - high.astype(F32)).astype(BF16)
+        return carry
+
+    lax.fori_loop(0, tiles, dg_body, 0)
+
+    for s in (1, 0, 3):
+        wait(along_core(s))
+    wct[...] = WC[...].reshape(1024, 128).T
+    biases = wct[80:96]
+    bias_ref[:, 0:512] = contract_last(biases, bias_places(0))
+    bias_ref[:, 512:1024] = contract_last(biases, bias_places(1))
+
+    def gated_copy(i):
+        return pltpu.make_async_copy(X.at[0, at(i)], gated_hbm.at[at(i)], st_g.at[i])
+
+    def forward_body(j, carry):
+        i = j % tiles
+
+        @pl.when(j == tiles)
+        def _():
+            @pl.when(dp > 0)
+            def _():
+                halo_copy.wait_recv()
+
+            put(0, halo[...])
+            lag_tile(i)
+
+        samples, lagged = X[1, at(i)], X[2, at(i)]
+        w0, w1 = W[0].reshape(512, 1024), W[1].reshape(512, 1024)
+        preact = matmul(lagged, w0) + matmul(samples, w1) + contract_first(condv[:, at(i)], wct[...])
+        a = jnp.tanh(preact[:, :512])
+        g = 0.5 * jnp.tanh(0.5 * preact[:, 512:]) + 0.5
+        X[0, at(i)] = (a * g).astype(BF16)
+        gated_copy(i).start()
+        dg = D[2, at(i)].astype(F32) + D[3, at(i)].astype(F32)
+        t = dg * g
+        D[2, at(i)] = (t * (1.0 - a * a)).astype(BF16)
+        D[3, at(i)] = (t * a * (1.0 - g)).astype(BF16)
+        return carry
+
+    lax.fori_loop(1, tiles + 1, forward_body, 0)
+
+    def back(i, s):
+        w = W[s].reshape(512, 1024)
+        return contract_last(D[2, at(i)], w[:, :512]) + contract_last(D[3, at(i)], w[:, 512:])
+
+    ret_send[...] = (back(0, 0) * keep(0)).astype(BF16)
+    ret_copy = rcopy(ret_send, ret_recv, h_s.at[1], h_r.at[1], (dp - 1, fs))
+
+    @pl.when(dp > 0)
+    def _():
+        ret_copy.start()
+
+    def stage0(k):
+        CS[k] = Gt[:, :, :, c1].astype(BF16)
+        GA[k] = Gt[:, :, :, c]
+        rcopy(CS.at[k], CR.at[k], rs_s.at[k, 0], rs_r.at[k, 0], sib).start()
+
+    def stage1(k):
+        rcopy(CS.at[k], CR.at[k], rs_s.at[k, 0], rs_r.at[k, 0], sib).wait()
+
+        @pl.when(k % 2 == 0)
+        def _():
+            S1[k] = (GA[k, :, :, y1] + CR[k, :, :, y1].astype(F32)).astype(BF16)
+            GA[k, :, :, y] += CR[k, :, :, y].astype(F32)
+            rcopy(S1.at[k], R1.at[k], rs_s.at[k, 1], rs_r.at[k, 1], yn).start()
+
+        @pl.when(k % 2 == 1)
+        def _():
+            S1[k] = (GA[k, :, x1] + CR[k, :, x1].astype(F32)).astype(BF16)
+            GA[k, :, x] += CR[k, :, x].astype(F32)
+            rcopy(S1.at[k], R1.at[k], rs_s.at[k, 1], rs_r.at[k, 1], xn).start()
+
+    def stage2(k):
+        rcopy(S1.at[k], R1.at[k], rs_s.at[k, 1], rs_r.at[k, 1], yn).wait()
+
+        @pl.when(k % 2 == 0)
+        def _():
+            S2[k] = (GA[k, :, x1, y] + R1[k, :, x1].astype(F32)).astype(BF16)
+            GA[k, :, x, y] += R1[k, :, x].astype(F32)
+            rcopy(S2.at[k], R2.at[k], rs_s.at[k, 2], rs_r.at[k, 2], xn).start()
+
+        @pl.when(k % 2 == 1)
+        def _():
+            S2[k] = (GA[k, :, x, y1] + R1[k, :, y1].astype(F32)).astype(BF16)
+            GA[k, :, x, y] += R1[k, :, y].astype(F32)
+            rcopy(S2.at[k], R2.at[k], rs_s.at[k, 2], rs_r.at[k, 2], yn).start()
+
+    def z_copies(k):
+        return [
+            rcopy(S3.at[k, zs[n]], R3.at[k, n], rs_s.at[k, 3 + n], rs_r.at[k, 3 + n], zn[n]) for n in range(3)
+        ]
+
+    def stage3(k):
+        rcopy(S2.at[k], R2.at[k], rs_s.at[k, 2], rs_r.at[k, 2], xn).wait()
+        total = GA[k, :, x, y] + R2[k].astype(F32)
+        GA[k, :, x, y] = total
+        S3[k] = total.astype(BF16)
+        start(z_copies(k))
+
+    def stage4(k):
+        wait(z_copies(k))
+        total = GA[k, z, x, y]
+        for n in range(3):
+            total = total + R3[k, n].astype(F32)
+        return total
+
+    def c0():
+        return rcopy(cCS, cCR, rs_s.at[6, 0], rs_r.at[6, 0], sib)
+
+    def c1_():
+        return rcopy(cS1, cR1, rs_s.at[6, 1], rs_r.at[6, 1], yn)
+
+    def c2():
+        return rcopy(cS2, cR2, rs_s.at[6, 2], rs_r.at[6, 2], xn)
+
+    def c3():
+        return [rcopy(cS3.at[zs[n]], cR3.at[n], rs_s.at[6, 3 + n], rs_r.at[6, 3 + n], zn[n]) for n in range(3)]
+
+    def cond_body(i, total):
+        return (
+            total[0] + matmul(condv[:, at(i)], D[2, at(i)]),
+            total[1] + matmul(condv[:, at(i)], D[3, at(i)]),
+        )
+
+    zero = jnp.zeros((128, 512), F32)
+    left, right = lax.fori_loop(0, tiles, cond_body, (zero, zero))
+
+    def sums_body(i, total):
+        return (
+            total[0] + jnp.sum(D[0, at(i)].astype(F32), axis=0, keepdims=True),
+            total[1] + jnp.sum(D[1, at(i)].astype(F32), axis=0, keepdims=True),
+        )
+
+    zero = jnp.zeros((1, 512), F32)
+    bres, bskip = lax.fori_loop(0, tiles, sums_body, (zero, zero))
+
+    def three_parts(value):
+        parts = []
+        for _ in range(3):
+            parts.append(value.astype(BF16))
+            value = value - parts[-1].astype(F32)
+        return jnp.concatenate(parts + [jnp.zeros((13, 512), BF16)], 0)
+
+    bias_row = matmul(three_parts(bres), bias_places(0)) + matmul(three_parts(bskip), bias_places(1))
+    bias_row = jnp.sum(bias_row, axis=0, keepdims=True)
+    grad_cond = jnp.concatenate([left, right], 1)
+    rows128 = lax.broadcasted_iota(jnp.int32, (128, 1024), 0)
+    grad_cond = jnp.where(rows128 == 81, bias_row, grad_cond)
+    gct = grad_cond.T.reshape(4, 2, 2, 2, 32, 128)
+    cGA[...] = gct
+    cCS[...] = cGA[:, :, :, c1]
+    c0().start()
+
+    def cond_stage1():
+        c0().wait()
+        cS1[...] = cGA[:, :, y1, c] + cCR[:, :, y1]
+        cGA[:, :, y, c] += cCR[:, :, y]
+        c1_().start()
+
+    def cond_stage2():
+        c1_().wait()
+        cS2[...] = cGA[:, x1, y, c] + cR1[:, x1]
+        cGA[:, x, y, c] += cR1[:, x]
+        c2().start()
+
+    def cond_stage3():
+        c2().wait()
+        total = cGA[:, x, y, c] + cR2[...]
+        cGA[:, x, y, c] = total
+        cS3[...] = total
+        start(c3())
+
+    def cond_stage4():
+        wait(c3())
+        total = cGA[z, x, y, c]
+        for n in range(3):
+            total = total + cR3[n]
+        gcond_ref[...] = total
+
+    def chunk_body(k, carry):
+        left, right = k // 2, k % 2 + 2 * ((k + 4) // 6)
+
+        def part(q, carry):
+            rows = pl.ds(pl.multiple_of(q * 1024, 1024), 1024)
+            prod = contract_first(X[left, rows], D[right, rows]).reshape(4, 2, 2, 2, 16, 512)
+
+            @pl.when(q == 0)
+            def _():
+                Gt[...] = prod
+
+            @pl.when(q > 0)
+            def _():
+                Gt[...] += prod
+
+            return carry
+
+        lax.fori_loop(0, T // 1024, part, 0)
+        stage0(k)
+
+        @pl.when(k >= 1)
+        def _():
+            stage1(k - 1)
+
+        @pl.when(k >= 3)
+        def _():
+            stage2(k - 3)
+
+        @pl.when(k >= 5)
+        def _():
+            stage3(k - 5)
+
+        @pl.when(k == 1)
+        def _():
+            cond_stage1()
+
+        @pl.when(k == 3)
+        def _():
+            cond_stage2()
+
+        @pl.when(k == 5)
+        def _():
+            cond_stage3()
+
+        return carry
+
+    lax.fori_loop(0, 6, chunk_body, 0)
+
+    @pl.when(dp < 7)
+    def _():
+        ret_copy.wait_recv()
+
+    put(0, ret_recv[...])
+
+    def e_copy(i):
+        return pltpu.make_async_copy(X.at[2, at(i)], e_hbm.at[at(i)], st_e.at[i])
+
+    def e_body(e, carry):
+        i = tiles - 1 - e
+        F[:, TILE : 2 * TILE] = F[:, 0:TILE]
+        put(0, back(i, 0) * keep(i))
+        X[2, at(i)] = (back(i, 1) + shifted(dilate)).astype(BF16)
+        e_copy(i).start()
+
+        @pl.when(e == 0)
+        def _():
+            stage1(5)
+            stage2(3)
+
+        @pl.when(e == 1)
+        def _():
+            stage3(1)
+
+        @pl.when(e == 2)
+        def _():
+            stage3(2)
+            stage2(4)
+
+        @pl.when(e == 4)
+        def _():
+            stage2(5)
+            stage3(3)
+
+        @pl.when(e == 6)
+        def _():
+            stage3(4)
+
+        return carry
+
+    lax.fori_loop(0, tiles, e_body, 0)
+    stage3(5)
+    cond_stage4()
+    for k in range(4):
+        gconv_ref[1 - k // 2, :, (k % 2) * 512 : (k % 2) * 512 + 512] = stage4(k + 2)
+    gres_ref[...] = stage4(0)
+    gskip_ref[...] = stage4(1)
+
+    def finish(i, carry):
+        gated_copy(i).wait()
+        e_copy(i).wait()
+        return carry
+
+    lax.fori_loop(0, tiles, finish, 0)
+    wrs_copy.wait()
+
+    @pl.when(dp < 7)
+    def _():
+        halo_copy.wait_send()
+
+    @pl.when(dp > 0)
+    def _():
+        ret_copy.wait_send()
+
+
+def output_kernel(gated_ref, sig_ref, e_ref, cot_ref, w_ref, bias_ref, res_ref, skip_ref, grad_ref):
+    gated, w = gated_ref[...], w_ref[...]
+    res = sig_ref[...].astype(F32) + matmul(gated, w[:, :512]) + bias_ref[1:2, 0:512]
+    res_ref[...] = res.astype(BF16)
+    skip_ref[...] = (matmul(gated, w[:, 512:]) + bias_ref[1:2, 512:1024]).astype(BF16)
+    grad_ref[...] = cot_ref[...].astype(F32) + e_ref[...].astype(F32)
+
+
+def shards(
+    signal, cond, clip_lengths, dilation, w_conv, w_cond, b_conv, w_res, b_res, w_skip, b_skip, cot_res, cot_skip
+):
+    T = signal.shape[1]
+    tiles = T // TILE
+    sig, conds, cr, cs = signal[0], cond[0], cot_res[0], cot_skip[0]
+    wb = jnp.concatenate(
+        [w_cond.T, b_conv[:, None], jnp.concatenate([b_res, b_skip])[:, None], jnp.zeros((32, 46), BF16)], 1
+    )
+    vmem, hbm, smem = (pl.BlockSpec(memory_space=m) for m in (pltpu.VMEM, pl.ANY, pltpu.SMEM))
+    dma = pltpu.SemaphoreType.DMA
+    out = jax.ShapeDtypeStruct
+    gated, e, wrs, bias, gconv, gres, gskip, gcond = pl.pallas_call(
+        layer_kernel,
+        out_shape=[
+            out((T, 512), BF16),
+            out((T, 512), BF16),
+            out((4, 2, 2, 2, 16, 1024), BF16),
+            out((16, 1024), F32),
+            out((2, 16, 1024), F32),
+            out((16, 512), F32),
+            out((16, 512), F32),
+            out((32, 128), F32),
+        ],
+        in_specs=[smem, smem] + [vmem] * 4 + [hbm] * 4,
+        out_specs=[hbm] * 3 + [vmem] * 5,
+        scratch_shapes=[
+            pltpu.VMEM((3, T, 512), BF16),
+            pltpu.VMEM((4, T, 512), BF16),
+            pltpu.VMEM((128, T), BF16),
+            pltpu.VMEM((3, 4, 2, 2, 2, 16, 1024), BF16),
+            pltpu.VMEM((4, 2, 2, 2, 32, 128), BF16),
+            pltpu.VMEM((128, 1024), BF16),
+            pltpu.VMEM((4, 2 * TILE, 128), F32),
+            pltpu.VMEM((DMAX, 512), BF16),
+            pltpu.VMEM((DMAX, 512), BF16),
+            pltpu.VMEM((DMAX, 512), BF16),
+            pltpu.VMEM((4, 2, 2, 2, 16, 512), F32),
+            pltpu.VMEM((6, 4, 2, 2, 16, 512), F32),
+            pltpu.VMEM((6, 4, 2, 2, 16, 512), BF16),
+            pltpu.VMEM((6, 4, 2, 2, 16, 512), BF16),
+            pltpu.VMEM((6, 4, 2, 16, 512), BF16),
+            pltpu.VMEM((6, 4, 2, 16, 512), BF16),
+            pltpu.VMEM((6, 4, 16, 512), BF16),
+            pltpu.VMEM((6, 4, 16, 512), BF16),
+            pltpu.VMEM((6, 4, 16, 512), BF16),
+            pltpu.VMEM((6, 3, 16, 512), BF16),
+            pltpu.VMEM((4, 2, 2, 2, 32, 128), F32),
+            pltpu.VMEM((4, 2, 2, 32, 128), F32),
+            pltpu.VMEM((4, 2, 2, 32, 128), F32),
+            pltpu.VMEM((4, 2, 32, 128), F32),
+            pltpu.VMEM((4, 2, 32, 128), F32),
+            pltpu.VMEM((4, 32, 128), F32),
+            pltpu.VMEM((4, 32, 128), F32),
+            pltpu.VMEM((4, 32, 128), F32),
+            pltpu.VMEM((3, 32, 128), F32),
+            dma((4,)),
+            dma((tiles,)),
+            dma((tiles,)),
+            dma((1,)),
+            dma((4, 8)),
+            dma((4, 8)),
+            dma((2,)),
+            dma((2,)),
+            dma((7, 6)),
+            dma((7, 6)),
+        ],
+        compiler_params=pltpu.CompilerParams(
+            collective_id=0, has_side_effects=True, vmem_limit_bytes=60 << 20
+        ),
+        name="layer",
+    )(clip_lengths, dilation, w_conv, w_res, w_skip, wb, sig, conds, cr, cs)
+
+    rows = pl.BlockSpec((TILE, 512), lambda i: (i, 0))
+    res_out, skip_out, grad_signal = pl.pallas_call(
+        output_kernel,
+        grid=(tiles,),
+        in_specs=[rows] * 4
+        + [pl.BlockSpec((512, 1024), lambda i: (0, 0)), pl.BlockSpec((16, 1024), lambda i: (0, 0))],
+        out_specs=[rows] * 3,
+        out_shape=[out((T, 512), BF16), out((T, 512), BF16), out((T, 512), F32)],
+        compiler_params=pltpu.CompilerParams(vmem_limit_bytes=60 << 20),
+        name="outputs",
+    )(gated, sig, e, cr, wrs.reshape(512, 1024), bias)
+    return (
+        res_out[None],
+        skip_out[None],
+        grad_signal[None],
+        gconv,
+        gcond[:, :80].T,
+        gcond[:, 80],
+        gres,
+        gcond[:16, 81],
+        gskip,
+        gcond[16:, 81],
+    )
 
 
 def from_behind(value, axis, steps):
@@ -12,23 +610,7 @@
     return lax.ppermute(value, axis, [(source, source + steps) for source in range(first, last)])
 
 
-def matmul(left, right):
-    return jnp.dot(left, right, preferred_element_type=jnp.float32)
-
-
-def contract_first(left, right):
-    return lax.dot_general(
-        left, right, (((0,), (0,)), ((), ())), preferred_element_type=jnp.float32
-    )
-
-
-def contract_last(left, right):
-    return lax.dot_general(
-        left, right, (((1,), (1,)), ((), ())), preferred_element_type=jnp.float32
-    )
-
-
-def shards(
+def shards_any(
     signal,
     cond,
     clip_lengths,
@@ -139,7 +721,7 @@
 
 def solution(mesh):
     return jax.shard_map(
-        shards,
+        shards if dict(mesh.shape) == {"dp": 8, "fsdp": 4} else shards_any,
         mesh=mesh,
         in_specs=(
             P("fsdp", "dp", None),

time: 810 us -> 130 us (0.16); the launches traced: 800 us -> 130 us
  waiting for transfers between devices: 383 us -> 0 us
  blocking collectives: 207 us -> 0 us
  matrix products: 134 us -> 0 us
  Pallas kernels: 0 us -> 122 us
  local copies, waits for them, and re-layouts: 36.3 us -> 4.83 us
  other arithmetic: 17 us -> 2.13 us
  between operations: 15.1 us -> 1.34 us
    reduce_scatter x3 -> x0, waiting for transfers between devices: 382 us -> none  [the longest x1 140 us: shards(): lax.psum_scatter(grad_conv, ('dp', 'fsdp'), scatter_dimension=1, tiled=True)]
    dot_general x14 -> x0, matrix products: 134 us -> none  [the longest x5 52.7 us: matmul(): return jnp.dot(left, right, preferred_element_type=jnp.float32)]
    pallas_call x0 -> x2, Pallas kernels: none -> 122 us  [the longest x1 106 us: shards(): pl.pallas_call(layer_kernel, out_shape=[out((T, 512), BF16), out((T, 512)...]
    all_gather x3 -> x0, blocking collectives: 121 us -> none  [the longest x1 42.3 us: shards(): lax.all_gather(w_skip, ('dp', 'fsdp'), axis=0, tiled=True)]
    unnamed x2 -> x0, blocking collectives: 86.1 us -> none
    dynamic_update_slice x1 -> x0, local copies, waits for them, and re-layouts: 22.1 us -> none  [shards(): lax.dynamic_update_slice_in_dim(d_extended, d_lagged, DMAX - dilate, 0)]
    reduce_sum x3 -> x0, other arithmetic: 11.2 us -> none  [the longest x1 4.66 us: shards(): grad_bconv = jnp.sum(d_preact.astype(jnp.float32), axis=0)]
  transfers between devices with their start and end apart: 7 -> 0, of which waited for: 3 -> 0; matrix products, arithmetic and copies ran while one was open for 18% -> 0% of each run, Pallas kernels for 0% -> 0%
where the time goes in v1:
time: 130 us
  Pallas kernels  122 us (94%)
  local copies, waits for them, and re-layouts  4.83 us (4%)
  other arithmetic  2.13 us (2%)
  between operations  1.34 us (1%)
    pallas_call x1, Pallas kernels, shards(): pl.pallas_call(layer_kernel, out_shape=[out((T, 512), BF16), out((T, 512)...  106 us
    pallas_call x1, Pallas kernels, shards(): pl.pallas_call(output_kernel, grid=(tiles,), in_specs=[rows] * 4 + [pl.Bl...  15.5 us

profile of v1, /device:TPU:0, one launch (start us, length us, event | category | flops | bytes accessed | tf_op | source)
XLA Modules:
  0.0 130.0 jit_solution(2186581014450623924)
XLA Ops:
  0.6 0.7 maximum_bitcast_fusion
  1.4 0.1 copy.26
  1.5 0.8 copy.25
  2.2 0.1 pad.3.clone
  2.3 1.4 %maximum_maximum_fusion.wb_ref = bf16[32,128]{1,0:T(8,128)(2,1)} fusion(bf16[32,1]{1,0:T(8,128)(2,1)S(1)} %copy.26, bf16[32,1]{1,0:T(8,128)(2,1)S(1)} %copy.25, bf16[32,80]{1,0:T(8,128)(2,1)} %bitcast.21, bf16[128]{0:T(256)(128)(2,1)S(1)} %pad.3.clone), kind=kLoop, calls=%fused_computation.2 | loop fusion | flops 32768 | bytes 13696 | tf_op jit(solution)/shard_map/concatenate | solution.py:515
  4.4 106.1 %layer.1 = (bf16[4096,512]{1,0:T(8,128)(2,1)}, bf16[4096,512]{1,0:T(8,128)(2,1)}, bf16[4,2,2,2,16,1024]{5,4,3,2,1,0:T(8,128)(2,1)}, f32[16,1024]{1,0:T(8,128)}, ...) custom-call(s32[1,16]{1,0:T(1,128)} %clip_ref.1, s32[1]{0:T(128)S(6)} %copy.30.dil_ref, ...), custom_call_target="tpu_custom_call" | custom-call | tf_op jit(solution)/shard_map/layer/pallas_call | solution.py:521
  110.5 0.0 copy-start
  110.5 0.0 copy-start.1
  110.5 0.0 copy-start.3
  110.5 0.0 copy-start.2
  110.5 15.5 %outputs.1 = (bf16[4096,512]{1,0:T(8,128)(2,1)}, bf16[4096,512]{1,0:T(8,128)(2,1)}, f32[4096,512]{1,0:T(8,128)}) custom-call(bf16[4096,512]{1,0:T(8,128)(2,1)} %get-tuple-element.21.gated_ref, bf16[4096,512]{1,0:T(8,128)(2,1)} %bitcast.15, bf16[4096,512]{1,0:T(8,128)(2,1)} %get-tuple-element.22.e_ref, bf16[4096,512]{1,0:T(8,128)(2,1)} %bitcast.17, ...), custom_call_target="tpu_custom_call" | custom-call | tf_op jit(solution)/shard_map/outputs/pallas_call | solution.py:583
  126.1 0.0 copy-done
  126.1 0.7 slice_reduce_fusion.1
  126.8 0.6 slice_bitcast_fusion
  127.4 0.7 slice_reduce_fusion
  128.1 0.0 copy-done.1
  128.1 0.7 copy.31
  128.7 0.0 copy-done.3
  128.7 0.6 copy.32
  129.3 0.0 copy-done.2
  129.3 0.6 copy.33
  (1 shorter events, 0.0 us)
Async XLA Ops:
  110.5 15.6 %copy-start = (f32[32,128]{1,0:T(8,128)S(1)}, f32[32,128]{1,0:T(8,128)}, u32[]{:S(2)}) copy-start(f32[32,128]{1,0:T(8,128)} %get-tuple-element.29) | copy-start | bytes 49156
  110.5 17.6 %copy-start.1 = (f32[2,16,1024]{2,1,0:T(8,128)S(1)}, f32[2,16,1024]{2,1,0:T(8,128)}, u32[]{:S(2)}) copy-start(f32[2,16,1024]{2,1,0:T(8,128)} %get-tuple-element.47) | copy-start | bytes 393220
  110.5 18.2 %copy-start.3 = (f32[16,512]{1,0:T(8,128)S(1)}, f32[16,512]{1,0:T(8,128)}, u32[]{:S(2)}) copy-start(f32[16,512]{1,0:T(8,128)} %get-tuple-element.50) | copy-start | bytes 98308
  110.5 18.8 %copy-start.2 = (f32[16,512]{1,0:T(8,128)S(1)}, f32[16,512]{1,0:T(8,128)}, u32[]{:S(2)}) copy-start(f32[16,512]{1,0:T(8,128)} %get-tuple-element.52) | copy-start | bytes 98308

commit v2 on v1

--- a/solution.py
+++ b/solution.py
@@ -9,6 +9,8 @@
 
 DMAX = 512
 TILE = 512
+BIG = 1024
+PIECES = 8
 MESH = pl.DeviceIdType.MESH
 BF16 = jnp.bfloat16
 F32 = jnp.float32
@@ -29,7 +31,7 @@
 def bias_places(skip):
     n = lax.broadcasted_iota(jnp.int32, (512, 1024), 0)
     m = lax.broadcasted_iota(jnp.int32, (512, 1024), 1)
-    place = (n // 16) * 32 + n % 16 + 16 * skip
+    place = ((n >> 4) << 5) + (n & 15) + 16 * skip
     return jnp.where(place == m, 1.0, 0.0).astype(BF16)
 
 
@@ -83,12 +85,14 @@
     def _():
         pl.semaphore_wait(barrier, 6)
 
-    W[0, z, x, y, c] = wconv_ref[0]
-    W[1, z, x, y, c] = wconv_ref[1]
+    for q in range(2):
+        for tap in range(2):
+            for n in range(2):
+                to = tap * 512 + n * 256
+                W[q, z, x, y, c, :, to : to + 256] = wconv_ref[tap, :, n * 512 + q * 256 : n * 512 + q * 256 + 256]
     W[2, z, x, y, c, :, 0:512] = wres_ref[...]
     W[2, z, x, y, c, :, 512:1024] = wskip_ref[...]
     WC[z, x, y, c] = wb_ref[...]
-    sections = (2, 1, 0, 3)
 
     def along_z(s):
         own = W.at[s, z, x, y, c] if s < 3 else WC.at[z, x, y, c]
@@ -118,16 +122,29 @@
         a = W.at[s, :, :, :, c] if s < 3 else WC.at[:, :, :, c]
         return [rcopy(a, a, ag_s.at[s, 7], ag_r.at[s, 7], sib)]
 
-    def start(copies):
-        for copy in copies:
-            copy.start()
-
-    def wait(copies):
-        for copy in copies:
-            copy.wait()
-
-    for s in sections:
-        start(along_z(s))
+    def start(phase, *sections):
+        for s in sections:
+            for copy in phase(s):
+                copy.start()
+
+    def wait(phase, *sections):
+        for s in sections:
+            for copy in phase(s):
+                copy.wait()
+
+    def halo_copy(n):
+        size = DMAX // PIECES
+        return rcopy(
+            X.at[1, pl.ds(T - DMAX + n * size, size)], halo.at[pl.ds(n * size, size)], h_s.at[n], h_r.at[n], (dp + 1, fs)
+        )
+
+    def send_halo(first, last):
+        @pl.when(dp < 7)
+        def _():
+            for n in range(first, last):
+                halo_copy(n).start()
+
+    start(along_z, 2)
 
     dilate = dil_ref[0]
     lane = lax.broadcasted_iota(jnp.int32, (1, 128), 1)
@@ -141,8 +158,8 @@
         inside = (starts <= times) & (starts > times - dilate)
         return 1.0 - jnp.max(jnp.where(inside, 1.0, 0.0), axis=1, keepdims=True)
 
-    def at(i):
-        return pl.ds(pl.multiple_of(i * TILE, TILE), TILE)
+    def at(i, size=TILE):
+        return pl.ds(pl.multiple_of(i * size, size), size)
 
     def put(half, value):
         for n in range(4):
@@ -154,183 +171,11 @@
     def lag_tile(i):
         put(1, X[1, at(i)])
         X[2, at(i)] = (shifted(TILE - dilate) * keep(i)).astype(BF16)
-
-    loads[0].wait()
 
     def lag_body(i, carry):
         put(0, X[1, at(i - 1)])
         lag_tile(i)
         return carry
-
-    lax.fori_loop(1, 3, lag_body, 0)
-    for s in sections:
-        wait(along_z(s))
-        start(along_one(s))
-    lax.fori_loop(3, 6, lag_body, 0)
-    for s in sections:
-        wait(along_one(s))
-        start(along_other(s))
-
-    halo_copy = rcopy(X.at[1, pl.ds(T - DMAX, DMAX)], halo, h_s.at[0], h_r.at[0], (dp + 1, fs))
-
-    @pl.when(dp < 7)
-    def _():
-        halo_copy.start()
-
-    @pl.when(dp == 0)
-    def _():
-        halo[...] = jnp.zeros_like(halo)
-
-    @pl.when(dp == 7)
-    def _():
-        ret_recv[...] = jnp.zeros_like(ret_recv)
-
-    lax.fori_loop(6, tiles, lag_body, 0)
-    condv[80:96] = jnp.where(lax.broadcasted_iota(jnp.int32, (16, T), 0) == 0, 1.0, 0.0).astype(BF16)
-    condv[96:128] = jnp.zeros((32, T), BF16)
-    for load in loads[1:]:
-        load.wait()
-    for s in sections:
-        wait(along_other(s))
-        start(along_core(s))
-
-    wait(along_core(2))
-    wrs_copy = pltpu.make_async_copy(W.at[2], wrs_hbm, st_w.at[0])
-    wrs_copy.start()
-    wrs = W[2].reshape(512, 1024)
-    wres, wskip = wrs[:, :512], wrs[:, 512:]
-
-    def dg_body(i, carry):
-        dg = contract_last(D[0, at(i)], wres) + contract_last(D[1, at(i)], wskip)
-        high = dg.astype(BF16)
-        D[2, at(i)] = high
-        D[3, at(i)] = (dg - high.astype(F32)).astype(BF16)
-        return carry
-
-    lax.fori_loop(0, tiles, dg_body, 0)
-
-    for s in (1, 0, 3):
-        wait(along_core(s))
-    wct[...] = WC[...].reshape(1024, 128).T
-    biases = wct[80:96]
-    bias_ref[:, 0:512] = contract_last(biases, bias_places(0))
-    bias_ref[:, 512:1024] = contract_last(biases, bias_places(1))
-
-    def gated_copy(i):
-        return pltpu.make_async_copy(X.at[0, at(i)], gated_hbm.at[at(i)], st_g.at[i])
-
-    def forward_body(j, carry):
-        i = j % tiles
-
-        @pl.when(j == tiles)
-        def _():
-            @pl.when(dp > 0)
-            def _():
-                halo_copy.wait_recv()
-
-            put(0, halo[...])
-            lag_tile(i)
-
-        samples, lagged = X[1, at(i)], X[2, at(i)]
-        w0, w1 = W[0].reshape(512, 1024), W[1].reshape(512, 1024)
-        preact = matmul(lagged, w0) + matmul(samples, w1) + contract_first(condv[:, at(i)], wct[...])
-        a = jnp.tanh(preact[:, :512])
-        g = 0.5 * jnp.tanh(0.5 * preact[:, 512:]) + 0.5
-        X[0, at(i)] = (a * g).astype(BF16)
-        gated_copy(i).start()
-        dg = D[2, at(i)].astype(F32) + D[3, at(i)].astype(F32)
-        t = dg * g
-        D[2, at(i)] = (t * (1.0 - a * a)).astype(BF16)
-        D[3, at(i)] = (t * a * (1.0 - g)).astype(BF16)
-        return carry
-
-    lax.fori_loop(1, tiles + 1, forward_body, 0)
-
-    def back(i, s):
-        w = W[s].reshape(512, 1024)
-        return contract_last(D[2, at(i)], w[:, :512]) + contract_last(D[3, at(i)], w[:, 512:])
-
-    ret_send[...] = (back(0, 0) * keep(0)).astype(BF16)
-    ret_copy = rcopy(ret_send, ret_recv, h_s.at[1], h_r.at[1], (dp - 1, fs))
-
-    @pl.when(dp > 0)
-    def _():
-        ret_copy.start()
-
-    def stage0(k):
-        CS[k] = Gt[:, :, :, c1].astype(BF16)
-        GA[k] = Gt[:, :, :, c]
-        rcopy(CS.at[k], CR.at[k], rs_s.at[k, 0], rs_r.at[k, 0], sib).start()
-
-    def stage1(k):
-        rcopy(CS.at[k], CR.at[k], rs_s.at[k, 0], rs_r.at[k, 0], sib).wait()
-
-        @pl.when(k % 2 == 0)
-        def _():
-            S1[k] = (GA[k, :, :, y1] + CR[k, :, :, y1].astype(F32)).astype(BF16)
-            GA[k, :, :, y] += CR[k, :, :, y].astype(F32)
-            rcopy(S1.at[k], R1.at[k], rs_s.at[k, 1], rs_r.at[k, 1], yn).start()
-
-        @pl.when(k % 2 == 1)
-        def _():
-            S1[k] = (GA[k, :, x1] + CR[k, :, x1].astype(F32)).astype(BF16)
-            GA[k, :, x] += CR[k, :, x].astype(F32)
-            rcopy(S1.at[k], R1.at[k], rs_s.at[k, 1], rs_r.at[k, 1], xn).start()
-
-    def stage2(k):
-        rcopy(S1.at[k], R1.at[k], rs_s.at[k, 1], rs_r.at[k, 1], yn).wait()
-
-        @pl.when(k % 2 == 0)
-        def _():
-            S2[k] = (GA[k, :, x1, y] + R1[k, :, x1].astype(F32)).astype(BF16)
-            GA[k, :, x, y] += R1[k, :, x].astype(F32)
-            rcopy(S2.at[k], R2.at[k], rs_s.at[k, 2], rs_r.at[k, 2], xn).start()
-
-        @pl.when(k % 2 == 1)
-        def _():
-            S2[k] = (GA[k, :, x, y1] + R1[k, :, y1].astype(F32)).astype(BF16)
-            GA[k, :, x, y] += R1[k, :, y].astype(F32)
-            rcopy(S2.at[k], R2.at[k], rs_s.at[k, 2], rs_r.at[k, 2], yn).start()
-
-    def z_copies(k):
-        return [
-            rcopy(S3.at[k, zs[n]], R3.at[k, n], rs_s.at[k, 3 + n], rs_r.at[k, 3 + n], zn[n]) for n in range(3)
-        ]
-
-    def stage3(k):
-        rcopy(S2.at[k], R2.at[k], rs_s.at[k, 2], rs_r.at[k, 2], xn).wait()
-        total = GA[k, :, x, y] + R2[k].astype(F32)
-        GA[k, :, x, y] = total
-        S3[k] = total.astype(BF16)
-        start(z_copies(k))
-
-    def stage4(k):
-        wait(z_copies(k))
-        total = GA[k, z, x, y]
-        for n in range(3):
-            total = total + R3[k, n].astype(F32)
-        return total
-
-    def c0():
-        return rcopy(cCS, cCR, rs_s.at[6, 0], rs_r.at[6, 0], sib)
-
-    def c1_():
-        return rcopy(cS1, cR1, rs_s.at[6, 1], rs_r.at[6, 1], yn)
-
-    def c2():
-        return rcopy(cS2, cR2, rs_s.at[6, 2], rs_r.at[6, 2], xn)
-
-    def c3():
-        return [rcopy(cS3.at[zs[n]], cR3.at[n], rs_s.at[6, 3 + n], rs_r.at[6, 3 + n], zn[n]) for n in range(3)]
-
-    def cond_body(i, total):
-        return (
-            total[0] + matmul(condv[:, at(i)], D[2, at(i)]),
-            total[1] + matmul(condv[:, at(i)], D[3, at(i)]),
-        )
-
-    zero = jnp.zeros((128, 512), F32)
-    left, right = lax.fori_loop(0, tiles, cond_body, (zero, zero))
 
     def sums_body(i, total):
         return (
@@ -338,8 +183,187 @@
             total[1] + jnp.sum(D[1, at(i)].astype(F32), axis=0, keepdims=True),
         )
 
+    def dg_body(i, carry):
+        wrs = W[2].reshape(512, 1024)
+        rows = at(i, BIG)
+        dg = contract_last(D[0, rows], wrs[:, :512]) + contract_last(D[1, rows], wrs[:, 512:])
+        high = dg.astype(BF16)
+        low = (dg - high.astype(F32)).astype(BF16)
+        for q in range(2):
+            D[2 + q, rows, 0:256] = high[:, q * 256 : q * 256 + 256]
+            D[2 + q, rows, 256:512] = low[:, q * 256 : q * 256 + 256]
+        return carry
+
+    loads[0].wait()
+    lax.fori_loop(1, 2, lag_body, 0)
+    wait(along_z, 2)
+    start(along_one, 2)
+    start(along_z, 0, 3, 1)
+    lax.fori_loop(2, 4, lag_body, 0)
+    wait(along_one, 2)
+    start(along_other, 2)
+    lax.fori_loop(4, 6, lag_body, 0)
+    wait(along_z, 0, 3)
+    start(along_one, 0, 3)
+    wait(along_z, 1)
+    start(along_one, 1)
+    lax.fori_loop(6, tiles, lag_body, 0)
+    wait(along_other, 2)
+    start(along_core, 2)
+    wait(along_one, 0, 3)
+    start(along_other, 0, 3)
+    wait(along_one, 1)
+    start(along_other, 1)
+    for load in loads[1:]:
+        load.wait()
     zero = jnp.zeros((1, 512), F32)
     bres, bskip = lax.fori_loop(0, tiles, sums_body, (zero, zero))
+    condv[80:96] = jnp.where(lax.broadcasted_iota(jnp.int32, (16, T), 0) == 0, 1.0, 0.0).astype(BF16)
+    condv[96:128] = jnp.zeros((32, T), BF16)
+    wait(along_core, 2)
+    wrs_copy = pltpu.make_async_copy(W.at[2], wrs_hbm, st_w.at[0])
+    wrs_copy.start()
+    lax.fori_loop(0, T // BIG // 2, dg_body, 0)
+    wait(along_other, 0, 3)
+    start(along_core, 0, 3)
+    lax.fori_loop(T // BIG // 2, T // BIG, dg_body, 0)
+    wait(along_other, 1)
+    start(along_core, 1)
+    send_halo(0, PIECES)
+
+    @pl.when(dp == 0)
+    def _():
+        halo[...] = jnp.zeros_like(halo)
+
+    @pl.when(dp == 7)
+    def _():
+        ret_recv[...] = jnp.zeros_like(ret_recv)
+
+    wait(along_core, 0, 3)
+    turned = WC[...].reshape(1024, 128).T
+    for q in range(2):
+        for n in range(2):
+            wct[q, :, n * 256 : n * 256 + 256] = turned[:, n * 512 + q * 256 : n * 512 + q * 256 + 256]
+    biases = turned[80:96]
+    bias_ref[:, 0:512] = contract_last(biases, bias_places(0))
+    bias_ref[:, 512:1024] = contract_last(biases, bias_places(1))
+
+    def forward(rows, q):
+        w = W[q].reshape(512, 1024)
+        preact = (
+            matmul(X[2, rows], w[:, :512])
+            + matmul(X[1, rows], w[:, 512:])
+            + contract_first(condv[:, rows], wct[q])
+        )
+        a = jnp.tanh(preact[:, :256])
+        g = 0.5 * jnp.tanh(0.5 * preact[:, 256:]) + 0.5
+        X[0, rows, q * 256 : q * 256 + 256] = (a * g).astype(BF16)
+        dg = D[2 + q, rows].astype(F32)
+        t = (dg[:, :256] + dg[:, 256:]) * g
+        D[2 + q, rows, 0:256] = (t * (1.0 - a * a)).astype(BF16)
+        D[2 + q, rows, 256:512] = (t * a * (1.0 - g)).astype(BF16)
+
+    def gated_copy(i):
+        return pltpu.make_async_copy(X.at[0, at(i)], gated_hbm.at[at(i)], st_g.at[i])
+
+    whole = (T - TILE) // BIG
+    for q in range(2):
+        if q == 1:
+            wait(along_core, 1)
+
+        def forward_body(j, carry, q=q):
+            forward(pl.ds(pl.multiple_of(TILE + j * BIG, TILE), BIG), q)
+            if q == 1:
+                for n in range(BIG // TILE):
+                    gated_copy(1 + j * (BIG // TILE) + n).start()
+            return carry
+
+        lax.fori_loop(0, whole, forward_body, 0)
+        for i in range(1 + whole * (BIG // TILE), tiles):
+            forward(at(i), q)
+            if q == 1:
+                gated_copy(i).start()
+
+    @pl.when(dp > 0)
+    def _():
+        for n in range(PIECES):
+            halo_copy(n).wait_recv()
+
+    put(0, halo[...])
+    lag_tile(0)
+    forward(at(0), 0)
+    forward(at(0), 1)
+    gated_copy(0).start()
+
+    def back(i, tap):
+        w0 = W[0].reshape(512, 1024)[:, tap * 512 : tap * 512 + 512]
+        w1 = W[1].reshape(512, 1024)[:, tap * 512 : tap * 512 + 512]
+        return contract_last(D[2, at(i)], w0) + contract_last(D[3, at(i)], w1)
+
+    first = back(0, 0) * keep(0)
+    put(0, first)
+    ret_send[...] = first.astype(BF16)
+
+    def ret_copy(n):
+        rows = pl.ds(pl.multiple_of(n * (DMAX // PIECES), DMAX // PIECES), DMAX // PIECES)
+        return rcopy(ret_send.at[rows], ret_recv.at[rows], h_s.at[PIECES + n], h_r.at[PIECES + n], (dp - 1, fs))
+
+    def send_back(n):
+        @pl.when(dp > 0)
+        def _():
+            ret_copy(n).start()
+
+    def to_core(k):
+        return rcopy(CS.at[k], CR.at[k], rs_s.at[k, 0], rs_r.at[k, 0], sib)
+
+    def to_first(k):
+        return rcopy(S1.at[k], R1.at[k], rs_s.at[k, 1], rs_r.at[k, 1], yn)
+
+    def to_second(k):
+        return rcopy(S2.at[k], R2.at[k], rs_s.at[k, 2], rs_r.at[k, 2], xn)
+
+    def to_z(k):
+        return [
+            rcopy(S3.at[k, zs[n]], R3.at[k, n], rs_s.at[k, 3 + n], rs_r.at[k, 3 + n], zn[n]) for n in range(3)
+        ]
+
+    def stage0(k):
+        CS[k] = Gt[:, :, :, c1].astype(BF16)
+        GA[k] = Gt[:, :, :, c]
+        to_core(k).start()
+
+    def stage1(k):
+        to_core(k).wait()
+        S1[k] = (GA[k, :, :, y1] + CR[k, :, :, y1].astype(F32)).astype(BF16)
+        to_first(k).start()
+        GA[k, :, :, y] += CR[k, :, :, y].astype(F32)
+
+    def stage2(k):
+        to_first(k).wait()
+        S2[k] = (GA[k, :, x1, y] + R1[k, :, x1].astype(F32)).astype(BF16)
+        to_second(k).start()
+        GA[k, :, x, y] += R1[k, :, x].astype(F32)
+
+    def stage3(k):
+        to_second(k).wait()
+        total = GA[k, :, x, y] + R2[k].astype(F32)
+        S3[k] = total.astype(BF16)
+        for copy in to_z(k):
+            copy.start()
+        GA[k, :, x, y] = total
+
+    def stage4(k):
+        for copy in to_z(k):
+            copy.wait()
+        total = GA[k, z, x, y]
+        for n in range(3):
+            total = total + R3[k, n].astype(F32)
+        return total
+
+    cond_core = rcopy(cCS, cCR, rs_s.at[6, 0], rs_r.at[6, 0], sib)
+    cond_first = rcopy(cS1, cR1, rs_s.at[6, 1], rs_r.at[6, 1], yn)
+    cond_second = rcopy(cS2, cR2, rs_s.at[6, 2], rs_r.at[6, 2], xn)
+    cond_z = [rcopy(cS3.at[zs[n]], cR3.at[n], rs_s.at[6, 3 + n], rs_r.at[6, 3 + n], zn[n]) for n in range(3)]
 
     def three_parts(value):
         parts = []
@@ -348,138 +372,106 @@
             value = value - parts[-1].astype(F32)
         return jnp.concatenate(parts + [jnp.zeros((13, 512), BF16)], 0)
 
-    bias_row = matmul(three_parts(bres), bias_places(0)) + matmul(three_parts(bskip), bias_places(1))
-    bias_row = jnp.sum(bias_row, axis=0, keepdims=True)
-    grad_cond = jnp.concatenate([left, right], 1)
-    rows128 = lax.broadcasted_iota(jnp.int32, (128, 1024), 0)
-    grad_cond = jnp.where(rows128 == 81, bias_row, grad_cond)
-    gct = grad_cond.T.reshape(4, 2, 2, 2, 32, 128)
-    cGA[...] = gct
-    cCS[...] = cGA[:, :, :, c1]
-    c0().start()
+    def cond_stage0():
+        bias_row = matmul(three_parts(bres), bias_places(0)) + matmul(three_parts(bskip), bias_places(1))
+        bias_row = jnp.sum(bias_row, axis=0, keepdims=True)
+        one, two = matmul(condv[...], D[2]), matmul(condv[...], D[3])
+        grad = jnp.concatenate([one[:, :256], two[:, :256], one[:, 256:], two[:, 256:]], 1)
+        place = lax.broadcasted_iota(jnp.int32, (128, 1024), 0)
+        cGA[...] = jnp.where(place == 81, bias_row, grad).T.reshape(4, 2, 2, 2, 32, 128)
+        cCS[...] = cGA[:, :, :, c1].astype(BF16)
+        cond_core.start()
 
     def cond_stage1():
-        c0().wait()
-        cS1[...] = cGA[:, :, y1, c] + cCR[:, :, y1]
-        cGA[:, :, y, c] += cCR[:, :, y]
-        c1_().start()
+        cond_core.wait()
+        cS1[...] = (cGA[:, :, y1, c] + cCR[:, :, y1].astype(F32)).astype(BF16)
+        cond_first.start()
+        cGA[:, :, y, c] += cCR[:, :, y].astype(F32)
 
     def cond_stage2():
-        c1_().wait()
-        cS2[...] = cGA[:, x1, y, c] + cR1[:, x1]
-        cGA[:, x, y, c] += cR1[:, x]
-        c2().start()
+        cond_first.wait()
+        cS2[...] = (cGA[:, x1, y, c] + cR1[:, x1].astype(F32)).astype(BF16)
+        cond_second.start()
+        cGA[:, x, y, c] += cR1[:, x].astype(F32)
 
     def cond_stage3():
-        c2().wait()
-        total = cGA[:, x, y, c] + cR2[...]
+        cond_second.wait()
+        total = cGA[:, x, y, c] + cR2[...].astype(F32)
+        cS3[...] = total.astype(BF16)
+        for copy in cond_z:
+            copy.start()
         cGA[:, x, y, c] = total
-        cS3[...] = total
-        start(c3())
 
     def cond_stage4():
-        wait(c3())
+        for copy in cond_z:
+            copy.wait()
         total = cGA[z, x, y, c]
         for n in range(3):
-            total = total + cR3[n]
+            total = total + cR3[n].astype(F32)
         gcond_ref[...] = total
+
+    def when(condition, work, *args):
+        @pl.when(condition)
+        def _():
+            work(*args)
+
+    cond_stage0()
 
     def chunk_body(k, carry):
         left, right = k // 2, k % 2 + 2 * ((k + 4) // 6)
-
-        def part(q, carry):
-            rows = pl.ds(pl.multiple_of(q * 1024, 1024), 1024)
-            prod = contract_first(X[left, rows], D[right, rows]).reshape(4, 2, 2, 2, 16, 512)
-
-            @pl.when(q == 0)
-            def _():
-                Gt[...] = prod
-
-            @pl.when(q > 0)
-            def _():
-                Gt[...] += prod
-
-            return carry
-
-        lax.fori_loop(0, T // 1024, part, 0)
+        Gt[...] = contract_first(X[left], D[right]).reshape(4, 2, 2, 2, 16, 512)
         stage0(k)
-
-        @pl.when(k >= 1)
-        def _():
-            stage1(k - 1)
-
-        @pl.when(k >= 3)
-        def _():
-            stage2(k - 3)
-
-        @pl.when(k >= 5)
-        def _():
-            stage3(k - 5)
-
-        @pl.when(k == 1)
-        def _():
-            cond_stage1()
-
-        @pl.when(k == 3)
-        def _():
-            cond_stage2()
-
-        @pl.when(k == 5)
-        def _():
-            cond_stage3()
-
+        when(k >= 1, stage1, k - 1)
+        when(k >= 3, stage2, k - 3)
+        when(k >= 5, stage3, k - 5)
+        when(k == 0, cond_stage1)
+        when(k == 2, cond_stage2)
+        when(k == 4, cond_stage3)
+        send_back(k)
         return carry
 
     lax.fori_loop(0, 6, chunk_body, 0)
+
+    def e_copy(i):
+        return pltpu.make_async_copy(X.at[2, at(i)], e_hbm.at[at(i)], st_e.at[i])
+
+    def e_tile(i):
+        X[2, at(i)] = (back(i, 1) + shifted(dilate)).astype(BF16)
+        e_copy(i).start()
+
+    def e_body(e, carry):
+        put(1, back(e + 1, 0) * keep(e + 1))
+        e_tile(e)
+        F[:, 0:TILE] = F[:, TILE : 2 * TILE]
+        when(e == 0, stage1, 5)
+        when(e == 0, stage2, 3)
+        when(e == 1, stage3, 1)
+        when(e == 1, stage2, 4)
+        when(e == 2, stage3, 2)
+        when(e == 3, stage2, 5)
+        when(e == 4, stage3, 3)
+        when(e == 5, stage3, 4)
+        when(e == 6, stage3, 5)
+        when(e < PIECES - 6, send_back, e + 6)
+        return carry
+
+    lax.fori_loop(0, tiles - 1, e_body, 0)
 
     @pl.when(dp < 7)
     def _():
-        ret_copy.wait_recv()
-
-    put(0, ret_recv[...])
-
-    def e_copy(i):
-        return pltpu.make_async_copy(X.at[2, at(i)], e_hbm.at[at(i)], st_e.at[i])
-
-    def e_body(e, carry):
-        i = tiles - 1 - e
-        F[:, TILE : 2 * TILE] = F[:, 0:TILE]
-        put(0, back(i, 0) * keep(i))
-        X[2, at(i)] = (back(i, 1) + shifted(dilate)).astype(BF16)
-        e_copy(i).start()
-
-        @pl.when(e == 0)
-        def _():
-            stage1(5)
-            stage2(3)
-
-        @pl.when(e == 1)
-        def _():
-            stage3(1)
-
-        @pl.when(e == 2)
-        def _():
-            stage3(2)
-            stage2(4)
-
-        @pl.when(e == 4)
-        def _():
-            stage2(5)
-            stage3(3)
-
-        @pl.when(e == 6)
-        def _():
-            stage3(4)
-
-        return carry
-
-    lax.fori_loop(0, tiles, e_body, 0)
-    stage3(5)
+        for n in range(PIECES):
+            ret_copy(n).wait_recv()
+
+    put(1, ret_recv[...])
+    e_tile(tiles - 1)
     cond_stage4()
-    for k in range(4):
-        gconv_ref[1 - k // 2, :, (k % 2) * 512 : (k % 2) * 512 + 512] = stage4(k + 2)
     gres_ref[...] = stage4(0)
     gskip_ref[...] = stage4(1)
+    for k in range(2, 6):
+        total, q = stage4(k), k % 2
+        for n in range(2):
+            to = n * 512 + q * 256
+            gconv_ref[1 - (k - 2) // 2, :, to : to + 256] = total[:, n * 256 : n * 256 + 256]
 
     def finish(i, carry):
         gated_copy(i).wait()
@@ -491,11 +483,13 @@
 
     @pl.when(dp < 7)
     def _():
-        halo_copy.wait_send()
+        for n in range(PIECES):
+            halo_copy(n).wait_send()
 
     @pl.when(dp > 0)
     def _():
-        ret_copy.wait_send()
+        for n in range(PIECES):
+            ret_copy(n).wait_send()
 
 
 def output_kernel(gated_ref, sig_ref, e_ref, cot_ref, w_ref, bias_ref, res_ref, skip_ref, grad_ref):
@@ -538,7 +532,7 @@
             pltpu.VMEM((128, T), BF16),
             pltpu.VMEM((3, 4, 2, 2, 2, 16, 1024), BF16),
             pltpu.VMEM((4, 2, 2, 2, 32, 128), BF16),
-            pltpu.VMEM((128, 1024), BF16),
+            pltpu.VMEM((2, 128, 512), BF16),
             pltpu.VMEM((4, 2 * TILE, 128), F32),
             pltpu.VMEM((DMAX, 512), BF16),
             pltpu.VMEM((DMAX, 512), BF16),
@@ -554,22 +548,22 @@
             pltpu.VMEM((6, 4, 16, 512), BF16),
             pltpu.VMEM((6, 3, 16, 512), BF16),
             pltpu.VMEM((4, 2, 2, 2, 32, 128), F32),
-            pltpu.VMEM((4, 2, 2, 32, 128), F32),
-            pltpu.VMEM((4, 2, 2, 32, 128), F32),
-            pltpu.VMEM((4, 2, 32, 128), F32),
-            pltpu.VMEM((4, 2, 32, 128), F32),
-            pltpu.VMEM((4, 32, 128), F32),
-            pltpu.VMEM((4, 32, 128), F32),
-            pltpu.VMEM((4, 32, 128), F32),
-            pltpu.VMEM((3, 32, 128), F32),
+            pltpu.VMEM((4, 2, 2, 32, 128), BF16),
+            pltpu.VMEM((4, 2, 2, 32, 128), BF16),
+            pltpu.VMEM((4, 2, 32, 128), BF16),
+            pltpu.VMEM((4, 2, 32, 128), BF16),
+            pltpu.VMEM((4, 32, 128), BF16),
+            pltpu.VMEM((4, 32, 128), BF16),
+            pltpu.VMEM((4, 32, 128), BF16),
+            pltpu.VMEM((3, 32, 128), BF16),
             dma((4,)),
             dma((tiles,)),
             dma((tiles,)),
             dma((1,)),
             dma((4, 8)),
             dma((4, 8)),
-            dma((2,)),
-            dma((2,)),
+            dma((2 * PIECES,)),
+            dma((2 * PIECES,)),
             dma((7, 6)),
             dma((7, 6)),
         ],

time: 130 us -> 107 us (0.82)
  Pallas kernels: 122 us -> 98.6 us
    pallas_call x1, Pallas kernels: 106 us -> 83.1 us  [shards(): pl.pallas_call(layer_kernel, out_shape=[out((T, 512), BF16), out((T, 512)...]
where the time goes in v2:
time: 107 us
  Pallas kernels  98.6 us (92%)
  local copies, waits for them, and re-layouts  4.83 us (5%)
  other arithmetic  2.13 us (2%)
  between operations  1.34 us (1%)
    pallas_call x1, Pallas kernels, shards(): pl.pallas_call(layer_kernel, out_shape=[out((T, 512), BF16), out((T, 512)...  83.1 us
    pallas_call x1, Pallas kernels, shards(): pl.pallas_call(output_kernel, grid=(tiles,), in_specs=[rows] * 4 + [pl.Bl...  15.5 us

profile of v2, /device:TPU:0, one launch (start us, length us, event | category | flops | bytes accessed | tf_op | source)
XLA Modules:
  0.0 106.9 jit_solution(15232788293936366562)
XLA Ops:
  0.6 0.7 maximum_bitcast_fusion
  1.4 0.1 copy.26
  1.5 0.8 copy.25
  2.2 0.1 pad.3.clone
  2.3 1.4 %maximum_maximum_fusion.wb_ref = bf16[32,128]{1,0:T(8,128)(2,1)} fusion(bf16[32,1]{1,0:T(8,128)(2,1)S(1)} %copy.26, bf16[32,1]{1,0:T(8,128)(2,1)S(1)} %copy.25, bf16[32,80]{1,0:T(8,128)(2,1)} %bitcast.21, bf16[128]{0:T(256)(128)(2,1)S(1)} %pad.3.clone), kind=kLoop, calls=%fused_computation.2 | loop fusion | flops 32768 | bytes 13696 | tf_op jit(solution)/shard_map/concatenate | solution.py:509
  4.4 83.1 %layer.1 = (bf16[4096,512]{1,0:T(8,128)(2,1)}, bf16[4096,512]{1,0:T(8,128)(2,1)}, bf16[4,2,2,2,16,1024]{5,4,3,2,1,0:T(8,128)(2,1)}, f32[16,1024]{1,0:T(8,128)}, ...) custom-call(s32[1,16]{1,0:T(1,128)} %clip_ref.1, s32[1]{0:T(128)S(6)} %copy.30.dil_ref, ...), custom_call_target="tpu_custom_call" | custom-call | tf_op jit(solution)/shard_map/layer/pallas_call | solution.py:515
  87.4 0.0 copy-start
  87.4 0.0 copy-start.1
  87.5 0.0 copy-start.3
  87.5 0.0 copy-start.2
  87.5 15.5 %outputs.1 = (bf16[4096,512]{1,0:T(8,128)(2,1)}, bf16[4096,512]{1,0:T(8,128)(2,1)}, f32[4096,512]{1,0:T(8,128)}) custom-call(bf16[4096,512]{1,0:T(8,128)(2,1)} %get-tuple-element.21.gated_ref, bf16[4096,512]{1,0:T(8,128)(2,1)} %bitcast.15, bf16[4096,512]{1,0:T(8,128)(2,1)} %get-tuple-element.22.e_ref, bf16[4096,512]{1,0:T(8,128)(2,1)} %bitcast.17, ...), custom_call_target="tpu_custom_call" | custom-call | tf_op jit(solution)/shard_map/outputs/pallas_call | solution.py:577
  103.0 0.0 copy-done
  103.0 0.7 slice_reduce_fusion.1
  103.7 0.6 slice_bitcast_fusion
  104.3 0.7 slice_reduce_fusion
  105.0 0.0 copy-done.1
  105.0 0.7 copy.31
  105.7 0.0 copy-done.3
  105.7 0.6 copy.32
  106.3 0.0 copy-done.2
  106.3 0.6 copy.33
  (1 shorter events, 0.0 us)
Async XLA Ops:
  87.4 15.6 %copy-start = (f32[32,128]{1,0:T(8,128)S(1)}, f32[32,128]{1,0:T(8,128)}, u32[]{:S(2)}) copy-start(f32[32,128]{1,0:T(8,128)} %get-tuple-element.29) | copy-start | bytes 49156
  87.4 17.6 %copy-start.1 = (f32[2,16,1024]{2,1,0:T(8,128)S(1)}, f32[2,16,1024]{2,1,0:T(8,128)}, u32[]{:S(2)}) copy-start(f32[2,16,1024]{2,1,0:T(8,128)} %get-tuple-element.47) | copy-start | bytes 393220
  87.5 18.2 %copy-start.3 = (f32[16,512]{1,0:T(8,128)S(1)}, f32[16,512]{1,0:T(8,128)}, u32[]{:S(2)}) copy-start(f32[16,512]{1,0:T(8,128)} %get-tuple-element.50) | copy-start | bytes 98308
  87.5 18.8 %copy-start.2 = (f32[16,512]{1,0:T(8,128)S(1)}, f32[16,512]{1,0:T(8,128)}, u32[]{:S(2)}) copy-start(f32[16,512]{1,0:T(8,128)} %get-tuple-element.52) | copy-start | bytes 98308

commit v3 on v2

--- a/solution.py
+++ b/solution.py
@@ -11,6 +11,8 @@
 TILE = 512
 BIG = 1024
 PIECES = 8
+SPLIT = 384
+OUT_TILE = 2048
 MESH = pl.DeviceIdType.MESH
 BF16 = jnp.bfloat16
 F32 = jnp.float32
@@ -36,10 +38,10 @@
 
 
 def layer_kernel(
-    clip_ref, dil_ref, wconv_ref, wres_ref, wskip_ref, wb_ref, sig_hbm, cond_hbm, cr_hbm, cs_hbm,
+    clip_ref, dil_ref, wconv_ref, wres_ref, wskip_ref, wcond_ref, bconv_ref, bres_ref, bskip_ref, sig_hbm, cond_hbm, cr_hbm, cs_hbm,
     gated_hbm, e_hbm, wrs_hbm, bias_ref, gconv_ref, gres_ref, gskip_ref, gcond_ref,
-    X, D, condv, W, WC, wct, F, halo, ret_send, ret_recv,
-    Gt, GA, CS, CR, S1, R1, S2, R2, S3, R3,
+    X, D, condv, W, WC, own_cond, wct, F, halo, ret_send, ret_recv,
+    Gt, GA, CS, CR, S1y, R1y, S1x, R1x, S2y, R2y, S2x, R2x, S3, R3,
     cGA, cCS, cCR, cS1, cR1, cS2, cR2, cS3, cR3,
     ld, st_g, st_e, st_w, ag_s, ag_r, h_s, h_r, rs_s, rs_r,
 ):
@@ -92,7 +94,18 @@
                 W[q, z, x, y, c, :, to : to + 256] = wconv_ref[tap, :, n * 512 + q * 256 : n * 512 + q * 256 + 256]
     W[2, z, x, y, c, :, 0:512] = wres_ref[...]
     W[2, z, x, y, c, :, 512:1024] = wskip_ref[...]
-    WC[z, x, y, c] = wb_ref[...]
+
+    def column(ref):
+        size = ref.shape[1]
+        square = jnp.broadcast_to(ref[...].astype(F32), (size, size))
+        diagonal = lax.broadcasted_iota(jnp.int32, (size, size), 0) == lax.broadcasted_iota(jnp.int32, (size, size), 1)
+        return jnp.sum(jnp.where(diagonal, square, 0.0), axis=1, keepdims=True)
+
+    own_cond[...] = jnp.zeros_like(own_cond)
+    own_cond[:, 0:80] = wcond_ref[...].astype(F32)
+    place = lax.broadcasted_iota(jnp.int32, (32, 128), 1)
+    pair = jnp.concatenate([column(bres_ref), column(bskip_ref)], 0)
+    WC[z, x, y, c] = jnp.where(place == 80, column(bconv_ref), jnp.where(place == 81, pair, own_cond[...])).astype(BF16)
 
     def along_z(s):
         own = W.at[s, z, x, y, c] if s < 3 else WC.at[z, x, y, c]
@@ -313,44 +326,66 @@
         def _():
             ret_copy(n).start()
 
+    send_back(0)
+    send_back(1)
+
     def to_core(k):
         return rcopy(CS.at[k], CR.at[k], rs_s.at[k, 0], rs_r.at[k, 0], sib)
 
     def to_first(k):
-        return rcopy(S1.at[k], R1.at[k], rs_s.at[k, 1], rs_r.at[k, 1], yn)
+        return [
+            rcopy(S1y.at[k], R1y.at[k], rs_s.at[k, 1], rs_r.at[k, 1], yn),
+            rcopy(S1x.at[k], R1x.at[k], rs_s.at[k, 2], rs_r.at[k, 2], xn),
+        ]
 
     def to_second(k):
-        return rcopy(S2.at[k], R2.at[k], rs_s.at[k, 2], rs_r.at[k, 2], xn)
+        return [
+            rcopy(S2y.at[k], R2y.at[k], rs_s.at[k, 3], rs_r.at[k, 3], xn),
+            rcopy(S2x.at[k], R2x.at[k], rs_s.at[k, 4], rs_r.at[k, 4], yn),
+        ]
 
     def to_z(k):
         return [
-            rcopy(S3.at[k, zs[n]], R3.at[k, n], rs_s.at[k, 3 + n], rs_r.at[k, 3 + n], zn[n]) for n in range(3)
+            rcopy(S3.at[k, zs[n]], R3.at[k, n], rs_s.at[k, 5 + n], rs_r.at[k, 5 + n], zn[n]) for n in range(3)
         ]
+
+    A, B = pl.ds(0, SPLIT), pl.ds(SPLIT, 512 - SPLIT)
 
     def stage0(k):
         CS[k] = Gt[:, :, :, c1].astype(BF16)
+        to_core(k).start()
         GA[k] = Gt[:, :, :, c]
-        to_core(k).start()
 
     def stage1(k):
         to_core(k).wait()
-        S1[k] = (GA[k, :, :, y1] + CR[k, :, :, y1].astype(F32)).astype(BF16)
-        to_first(k).start()
-        GA[k, :, :, y] += CR[k, :, :, y].astype(F32)
+        S1y[k] = (GA[k, :, :, y1, :, A] + CR[k, :, :, y1, :, A].astype(F32)).astype(BF16)
+        S1x[k] = (GA[k, :, x1, :, :, B] + CR[k, :, x1, :, :, B].astype(F32)).astype(BF16)
+        for copy in to_first(k):
+            copy.start()
+        GA[k, :, :, y, :, A] += CR[k, :, :, y, :, A].astype(F32)
+        GA[k, :, x, :, :, B] += CR[k, :, x, :, :, B].astype(F32)
 
     def stage2(k):
-        to_first(k).wait()
-        S2[k] = (GA[k, :, x1, y] + R1[k, :, x1].astype(F32)).astype(BF16)
-        to_second(k).start()
-        GA[k, :, x, y] += R1[k, :, x].astype(F32)
+        for copy in to_first(k):
+            copy.wait()
+        S2y[k] = (GA[k, :, x1, y, :, A] + R1y[k, :, x1].astype(F32)).astype(BF16)
+        S2x[k] = (GA[k, :, x, y1, :, B] + R1x[k, :, y1].astype(F32)).astype(BF16)
+        for copy in to_second(k):
+            copy.start()
+        GA[k, :, x, y, :, A] += R1y[k, :, x].astype(F32)
+        GA[k, :, x, y, :, B] += R1x[k, :, y].astype(F32)
 
     def stage3(k):
-        to_second(k).wait()
-        total = GA[k, :, x, y] + R2[k].astype(F32)
-        S3[k] = total.astype(BF16)
+        for copy in to_second(k):
+            copy.wait()
+        one = GA[k, :, x, y, :, A] + R2y[k].astype(F32)
+        two = GA[k, :, x, y, :, B] + R2x[k].astype(F32)
+        S3[k, :, :, A] = one.astype(BF16)
+        S3[k, :, :, B] = two.astype(BF16)
         for copy in to_z(k):
             copy.start()
-        GA[k, :, x, y] = total
+        GA[k, :, x, y, :, A] = one
+        GA[k, :, x, y, :, B] = two
 
     def stage4(k):
         for copy in to_z(k):
@@ -427,7 +462,7 @@
         when(k == 0, cond_stage1)
         when(k == 2, cond_stage2)
         when(k == 4, cond_stage3)
-        send_back(k)
+        send_back(k + 2)
         return carry
 
     lax.fori_loop(0, 6, chunk_body, 0)
@@ -449,10 +484,9 @@
         when(e == 1, stage2, 4)
         when(e == 2, stage3, 2)
         when(e == 3, stage2, 5)
-        when(e == 4, stage3, 3)
-        when(e == 5, stage3, 4)
-        when(e == 6, stage3, 5)
-        when(e < PIECES - 6, send_back, e + 6)
+        when(e == 3, stage3, 3)
+        when(e == 4, stage3, 4)
+        when(e == 5, stage3, 5)
         return carry
 
     lax.fori_loop(0, tiles - 1, e_body, 0)
@@ -492,12 +526,33 @@
             ret_copy(n).wait_send()
 
 
-def output_kernel(gated_ref, sig_ref, e_ref, cot_ref, w_ref, bias_ref, res_ref, skip_ref, grad_ref):
+def output_kernel(
+    gated_ref, sig_ref, e_ref, cot_ref, w_ref, bias_ref, gconv_ref, gres_ref, gskip_ref, gcond_ref,
+    res_ref, skip_ref, grad_ref, conv_out, res_out, skip_out, cond_out, bconv_out, bres_out, bskip_out,
+):
     gated, w = gated_ref[...], w_ref[...]
     res = sig_ref[...].astype(F32) + matmul(gated, w[:, :512]) + bias_ref[1:2, 0:512]
     res_ref[...] = res.astype(BF16)
     skip_ref[...] = (matmul(gated, w[:, 512:]) + bias_ref[1:2, 512:1024]).astype(BF16)
     grad_ref[...] = cot_ref[...].astype(F32) + e_ref[...].astype(F32)
+
+    @pl.when(pl.program_id(0) == 0)
+    def _():
+        conv_out[...] = gconv_ref[...]
+        res_out[...] = gres_ref[...]
+        skip_out[...] = gskip_ref[...]
+        cond_out[...] = gcond_ref[:, 0:80]
+
+        def as_row(value):
+            size = value.shape[0]
+            square = jnp.broadcast_to(value, (size, size))
+            first = lax.broadcasted_iota(jnp.int32, (size, size), 0)
+            second = lax.broadcasted_iota(jnp.int32, (size, size), 1)
+            return jnp.sum(jnp.where(first == second, square, 0.0), axis=0, keepdims=True)
+
+        bconv_out[...] = as_row(gcond_ref[:, 80:81])
+        bres_out[...] = as_row(gcond_ref[0:16, 81:82])
+        bskip_out[...] = as_row(gcond_ref[16:32, 81:82])
 
 
 def shards(
@@ -506,9 +561,6 @@
     T = signal.shape[1]
     tiles = T // TILE
     sig, conds, cr, cs = signal[0], cond[0], cot_res[0], cot_skip[0]
-    wb = jnp.concatenate(
-        [w_cond.T, b_conv[:, None], jnp.concatenate([b_res, b_skip])[:, None], jnp.zeros((32, 46), BF16)], 1
-    )
     vmem, hbm, smem = (pl.BlockSpec(memory_space=m) for m in (pltpu.VMEM, pl.ANY, pltpu.SMEM))
     dma = pltpu.SemaphoreType.DMA
     out = jax.ShapeDtypeStruct
@@ -524,7 +576,7 @@
             out((16, 512), F32),
             out((32, 128), F32),
         ],
-        in_specs=[smem, smem] + [vmem] * 4 + [hbm] * 4,
+        in_specs=[smem, smem] + [vmem] * 7 + [hbm] * 4,
         out_specs=[hbm] * 3 + [vmem] * 5,
         scratch_shapes=[
             pltpu.VMEM((3, T, 512), BF16),
@@ -532,6 +584,7 @@
             pltpu.VMEM((128, T), BF16),
             pltpu.VMEM((3, 4, 2, 2, 2, 16, 1024), BF16),
             pltpu.VMEM((4, 2, 2, 2, 32, 128), BF16),
+            pltpu.VMEM((32, 128), F32),
             pltpu.VMEM((2, 128, 512), BF16),
             pltpu.VMEM((4, 2 * TILE, 128), F32),
             pltpu.VMEM((DMAX, 512), BF16),
@@ -541,10 +594,14 @@
             pltpu.VMEM((6, 4, 2, 2, 16, 512), F32),
             pltpu.VMEM((6, 4, 2, 2, 16, 512), BF16),
             pltpu.VMEM((6, 4, 2, 2, 16, 512), BF16),
-            pltpu.VMEM((6, 4, 2, 16, 512), BF16),
-            pltpu.VMEM((6, 4, 2, 16, 512), BF16),
-            pltpu.VMEM((6, 4, 16, 512), BF16),
-            pltpu.VMEM((6, 4, 16, 512), BF16),
+            pltpu.VMEM((6, 4, 2, 16, SPLIT), BF16),
+            pltpu.VMEM((6, 4, 2, 16, SPLIT), BF16),
+            pltpu.VMEM((6, 4, 2, 16, 512 - SPLIT), BF16),
+            pltpu.VMEM((6, 4, 2, 16, 512 - SPLIT), BF16),
+            pltpu.VMEM((6, 4, 16, SPLIT), BF16),
+            pltpu.VMEM((6, 4, 16, SPLIT), BF16),
+            pltpu.VMEM((6, 4, 16, 512 - SPLIT), BF16),
+            pltpu.VMEM((6, 4, 16, 512 - SPLIT), BF16),
             pltpu.VMEM((6, 4, 16, 512), BF16),
             pltpu.VMEM((6, 3, 16, 512), BF16),
             pltpu.VMEM((4, 2, 2, 2, 32, 128), F32),
@@ -564,37 +621,44 @@
             dma((4, 8)),
             dma((2 * PIECES,)),
             dma((2 * PIECES,)),
-            dma((7, 6)),
-            dma((7, 6)),
+            dma((7, 8)),
+            dma((7, 8)),
         ],
         compiler_params=pltpu.CompilerParams(
             collective_id=0, has_side_effects=True, vmem_limit_bytes=60 << 20
         ),
         name="layer",
-    )(clip_lengths, dilation, w_conv, w_res, w_skip, wb, sig, conds, cr, cs)
-
-    rows = pl.BlockSpec((TILE, 512), lambda i: (i, 0))
-    res_out, skip_out, grad_signal = pl.pallas_call(
+    )(
+        clip_lengths, dilation, w_conv, w_res, w_skip, w_cond.T, b_conv[None], b_res[None], b_skip[None], sig, conds, cr, cs
+    )
+
+    rows = pl.BlockSpec((OUT_TILE, 512), lambda i: (i, 0))
+
+    def whole(array):
+        return pl.BlockSpec(array.shape, lambda i: (0,) * len(array.shape))
+
+    small = [wrs.reshape(512, 1024), bias, gconv, gres, gskip, gcond]
+    sums = [out(g.shape, F32) for g in (gconv, gres, gskip)] + [out(shape, F32) for shape in ((32, 80), (1, 32), (1, 16), (1, 16))]
+    res_out, skip_out, grad_signal, gconv, gres, gskip, gcond, gbconv, gbres, gbskip = pl.pallas_call(
         output_kernel,
-        grid=(tiles,),
-        in_specs=[rows] * 4
-        + [pl.BlockSpec((512, 1024), lambda i: (0, 0)), pl.BlockSpec((16, 1024), lambda i: (0, 0))],
-        out_specs=[rows] * 3,
-        out_shape=[out((T, 512), BF16), out((T, 512), BF16), out((T, 512), F32)],
+        grid=(T // OUT_TILE,),
+        in_specs=[rows] * 4 + [whole(array) for array in small],
+        out_specs=[rows] * 3 + [whole(array) for array in sums],
+        out_shape=[out((T, 512), BF16), out((T, 512), BF16), out((T, 512), F32)] + sums,
         compiler_params=pltpu.CompilerParams(vmem_limit_bytes=60 << 20),
         name="outputs",
-    )(gated, sig, e, cr, wrs.reshape(512, 1024), bias)
+    )(gated, sig, e, cr, *small)
     return (
         res_out[None],
         skip_out[None],
         grad_signal[None],
         gconv,
-        gcond[:, :80].T,
-        gcond[:, 80],
+        gcond.T,
+        gbconv[0],
         gres,
-        gcond[:16, 81],
+        gbres[0],
         gskip,
-        gcond[16:, 81],
+        gbskip[0],
     )
 
 

time: 107 us -> 96.8 us (0.905)
  local copies, waits for them, and re-layouts: 4.83 us -> 0 us
  Pallas kernels: 98.6 us -> 95.2 us
  other arithmetic: 2.13 us -> 0 us
    pallas_call x1, Pallas kernels: 83.1 us -> 81.1 us  [shards(): pl.pallas_call(layer_kernel, out_shape=[out((T, 512), BF16), out((T, 512)...]
    unnamed x11 -> x0, local copies, waits for them, and re-layouts: 1.9 us -> none
    pallas_call x1, Pallas kernels: 15.5 us -> 14.1 us  [shards(): pl.pallas_call(output_kernel, grid=(T // OUT_TILE,), in_specs=[rows] * 4...]
    slice x2 -> x0, local copies, waits for them, and re-layouts: 1.39 us -> none  [the longest x1 0.7 us: shards(): gcond[16:, 81]]
    concatenate x1 -> x0, other arithmetic: 1.38 us -> none  [shards(): jnp.concatenate([w_cond.T, b_conv[:, None], jnp.concatenate([b_res, b_ski...]
where the time goes in v3:
time: 96.8 us; the launch traced here: 96.7 us
  Pallas kernels  95.2 us (98%)
  between operations  1.48 us (2%)
    pallas_call x1, Pallas kernels, shards(): pl.pallas_call(layer_kernel, out_shape=[out((T, 512), BF16), out((T, 512)...  81.1 us
    pallas_call x1, Pallas kernels, shards(): pl.pallas_call(output_kernel, grid=(T // OUT_TILE,), in_specs=[rows] * 4...  14.1 us

profile of v3, /device:TPU:0, one launch (start us, length us, event | category | flops | bytes accessed | tf_op | source)
XLA Modules:
  0.0 96.7 jit_solution(854760068874786897)
XLA Ops:
  1.3 81.1 %layer.1 = (bf16[4096,512]{1,0:T(8,128)(2,1)}, bf16[4096,512]{1,0:T(8,128)(2,1)}, bf16[4,2,2,2,16,1024]{5,4,3,2,1,0:T(8,128)(2,1)}, f32[16,1024]{1,0:T(8,128)}, ...) custom-call(s32[1,16]{1,0:T(1,128)} %clip_ref.1, s32[1]{0:T(128)S(6)} %copy.23.dil_ref, ...), custom_call_target="tpu_custom_call" | custom-call | tf_op jit(solution)/shard_map/layer/pallas_call | solution.py:567
  82.4 14.1 %outputs.1 = (bf16[4096,512]{1,0:T(8,128)(2,1)}, bf16[4096,512]{1,0:T(8,128)(2,1)}, f32[4096,512]{1,0:T(8,128)}, f32[2,16,1024]{2,1,0:T(8,128)}, f32[16,512]{1,0...) custom-call(bf16[4096,512]{1,0:T(8,128)(2,1)} %get-tuple-element.28., ...), custom_call_target="tpu_custom_call" | custom-call | tf_op jit(solution)/shard_map/outputs/pallas_call | solution.py:642

commit v4 on v3

--- a/solution.py
+++ b/solution.py
@@ -172,7 +172,7 @@
         return 1.0 - jnp.max(jnp.where(inside, 1.0, 0.0), axis=1, keepdims=True)
 
     def at(i, size=TILE):
-        return pl.ds(pl.multiple_of(i * size, size), size)
+        return pl.ds(i * size if isinstance(i, int) else pl.multiple_of(i * size, size), size)
 
     def put(half, value):
         for n in range(4):
@@ -196,16 +196,14 @@
             total[1] + jnp.sum(D[1, at(i)].astype(F32), axis=0, keepdims=True),
         )
 
-    def dg_body(i, carry):
+    def d_gated(rows):
         wrs = W[2].reshape(512, 1024)
-        rows = at(i, BIG)
         dg = contract_last(D[0, rows], wrs[:, :512]) + contract_last(D[1, rows], wrs[:, 512:])
         high = dg.astype(BF16)
         low = (dg - high.astype(F32)).astype(BF16)
         for q in range(2):
             D[2 + q, rows, 0:256] = high[:, q * 256 : q * 256 + 256]
             D[2 + q, rows, 256:512] = low[:, q * 256 : q * 256 + 256]
-        return carry
 
     loads[0].wait()
     lax.fori_loop(1, 2, lag_body, 0)
@@ -215,12 +213,11 @@
     lax.fori_loop(2, 4, lag_body, 0)
     wait(along_one, 2)
     start(along_other, 2)
-    lax.fori_loop(4, 6, lag_body, 0)
     wait(along_z, 0, 3)
     start(along_one, 0, 3)
     wait(along_z, 1)
     start(along_one, 1)
-    lax.fori_loop(6, tiles, lag_body, 0)
+    lax.fori_loop(4, tiles, lag_body, 0)
     wait(along_other, 2)
     start(along_core, 2)
     wait(along_one, 0, 3)
@@ -236,6 +233,10 @@
     wait(along_core, 2)
     wrs_copy = pltpu.make_async_copy(W.at[2], wrs_hbm, st_w.at[0])
     wrs_copy.start()
+    def dg_body(i, carry):
+        d_gated(at(i, BIG))
+        return carry
+
     lax.fori_loop(0, T // BIG // 2, dg_body, 0)
     wait(along_other, 0, 3)
     start(along_core, 0, 3)
@@ -291,7 +292,8 @@
                     gated_copy(1 + j * (BIG // TILE) + n).start()
             return carry
 
-        lax.fori_loop(0, whole, forward_body, 0)
+        lax.fori_loop(0, 1, forward_body, 0)
+        lax.fori_loop(1, whole, forward_body, 0)
         for i in range(1 + whole * (BIG // TILE), tiles):
             forward(at(i), q)
             if q == 1:
@@ -450,8 +452,6 @@
         def _():
             work(*args)
 
-    cond_stage0()
-
     def chunk_body(k, carry):
         left, right = k // 2, k % 2 + 2 * ((k + 4) // 6)
         Gt[...] = contract_first(X[left], D[right]).reshape(4, 2, 2, 2, 16, 512)
@@ -459,34 +459,35 @@
         when(k >= 1, stage1, k - 1)
         when(k >= 3, stage2, k - 3)
         when(k >= 5, stage3, k - 5)
-        when(k == 0, cond_stage1)
-        when(k == 2, cond_stage2)
-        when(k == 4, cond_stage3)
         send_back(k + 2)
         return carry
 
     lax.fori_loop(0, 6, chunk_body, 0)
+    cond_stage0()
+    stage1(5)
+    stage2(3)
 
     def e_copy(i):
         return pltpu.make_async_copy(X.at[2, at(i)], e_hbm.at[at(i)], st_e.at[i])
 
     def e_tile(i):
-        X[2, at(i)] = (back(i, 1) + shifted(dilate)).astype(BF16)
+        X[2, at(i)] = (D[0, at(i)].astype(F32) + back(i, 1) + shifted(dilate)).astype(BF16)
         e_copy(i).start()
 
     def e_body(e, carry):
         put(1, back(e + 1, 0) * keep(e + 1))
         e_tile(e)
         F[:, 0:TILE] = F[:, TILE : 2 * TILE]
-        when(e == 0, stage1, 5)
-        when(e == 0, stage2, 3)
-        when(e == 1, stage3, 1)
+        when(e == 0, stage3, 1)
         when(e == 1, stage2, 4)
-        when(e == 2, stage3, 2)
-        when(e == 3, stage2, 5)
-        when(e == 3, stage3, 3)
-        when(e == 4, stage3, 4)
-        when(e == 5, stage3, 5)
+        when(e == 1, stage3, 2)
+        when(e == 1, cond_stage1)
+        when(e == 2, stage2, 5)
+        when(e == 2, stage3, 3)
+        when(e == 3, stage3, 4)
+        when(e == 3, cond_stage2)
+        when(e == 4, stage3, 5)
+        when(e == 5, cond_stage3)
         return carry
 
     lax.fori_loop(0, tiles - 1, e_body, 0)
@@ -527,14 +528,14 @@
 
 
 def output_kernel(
-    gated_ref, sig_ref, e_ref, cot_ref, w_ref, bias_ref, gconv_ref, gres_ref, gskip_ref, gcond_ref,
+    gated_ref, sig_ref, e_ref, w_ref, bias_ref, gconv_ref, gres_ref, gskip_ref, gcond_ref,
     res_ref, skip_ref, grad_ref, conv_out, res_out, skip_out, cond_out, bconv_out, bres_out, bskip_out,
 ):
     gated, w = gated_ref[...], w_ref[...]
     res = sig_ref[...].astype(F32) + matmul(gated, w[:, :512]) + bias_ref[1:2, 0:512]
     res_ref[...] = res.astype(BF16)
     skip_ref[...] = (matmul(gated, w[:, 512:]) + bias_ref[1:2, 512:1024]).astype(BF16)
-    grad_ref[...] = cot_ref[...].astype(F32) + e_ref[...].astype(F32)
+    grad_ref[...] = e_ref[...].astype(F32)
 
     @pl.when(pl.program_id(0) == 0)
     def _():
@@ -642,12 +643,12 @@
     res_out, skip_out, grad_signal, gconv, gres, gskip, gcond, gbconv, gbres, gbskip = pl.pallas_call(
         output_kernel,
         grid=(T // OUT_TILE,),
-        in_specs=[rows] * 4 + [whole(array) for array in small],
+        in_specs=[rows] * 3 + [whole(array) for array in small],
         out_specs=[rows] * 3 + [whole(array) for array in sums],
         out_shape=[out((T, 512), BF16), out((T, 512), BF16), out((T, 512), F32)] + sums,
         compiler_params=pltpu.CompilerParams(vmem_limit_bytes=60 << 20),
         name="outputs",
-    )(gated, sig, e, cr, *small)
+    )(gated, sig, e, *small)
     return (
         res_out[None],
         skip_out[None],

time: 96.8 us -> 95 us (0.981)
  Pallas kernels: 95.2 us -> 93.4 us
    pallas_call x1, Pallas kernels: 14.1 us -> 12.5 us  [shards(): pl.pallas_call(output_kernel, grid=(T // OUT_TILE,), in_specs=[rows] * 3...]
where the time goes in v4:
time: 95 us; the launch traced here: 94.9 us
  Pallas kernels  93.4 us (98%)
  between operations  1.44 us (2%)
    pallas_call x1, Pallas kernels, shards(): pl.pallas_call(layer_kernel, out_shape=[out((T, 512), BF16), out((T, 512)...  80.9 us
    pallas_call x1, Pallas kernels, shards(): pl.pallas_call(output_kernel, grid=(T // OUT_TILE,), in_specs=[rows] * 3...  12.5 us

profile of v4, /device:TPU:0, one launch (start us, length us, event | category | flops | bytes accessed | tf_op | source)
XLA Modules:
  0.0 94.9 jit_solution(10699665378970356435)
XLA Ops:
  1.3 80.9 %layer.1 = (bf16[4096,512]{1,0:T(8,128)(2,1)}, bf16[4096,512]{1,0:T(8,128)(2,1)}, bf16[4,2,2,2,16,1024]{5,4,3,2,1,0:T(8,128)(2,1)}, f32[16,1024]{1,0:T(8,128)}, ...) custom-call(s32[1,16]{1,0:T(1,128)} %clip_ref.1, s32[1]{0:T(128)S(6)} %copy.23.dil_ref, ...), custom_call_target="tpu_custom_call" | custom-call | tf_op jit(solution)/shard_map/layer/pallas_call | solution.py:568
  82.2 12.5 %outputs.1 = (bf16[4096,512]{1,0:T(8,128)(2,1)}, bf16[4096,512]{1,0:T(8,128)(2,1)}, f32[4096,512]{1,0:T(8,128)}, f32[2,16,1024]{2,1,0:T(8,128)}, f32[16,512]{1,0...) custom-call(bf16[4096,512]{1,0:T(8,128)(2,1)} %get-tuple-element.28., ...), custom_call_target="tpu_custom_call" | custom-call | tf_op jit(solution)/shard_map/outputs/pallas_call | solution.py:643

commit v5 on v4

--- a/solution.py
+++ b/solution.py
@@ -278,7 +278,7 @@
         D[2 + q, rows, 256:512] = (t * a * (1.0 - g)).astype(BF16)
 
     def gated_copy(i):
-        return pltpu.make_async_copy(X.at[0, at(i)], gated_hbm.at[at(i)], st_g.at[i])
+        return pltpu.make_async_copy(X.at[0, at(i)], gated_hbm.at[at(i)], st_g.at[0])
 
     whole = (T - TILE) // BIG
     for q in range(2):
@@ -468,7 +468,7 @@
     stage2(3)
 
     def e_copy(i):
-        return pltpu.make_async_copy(X.at[2, at(i)], e_hbm.at[at(i)], st_e.at[i])
+        return pltpu.make_async_copy(X.at[2, at(i)], e_hbm.at[at(i)], st_e.at[0])
 
     def e_tile(i):
         X[2, at(i)] = (D[0, at(i)].astype(F32) + back(i, 1) + shifted(dilate)).astype(BF16)
@@ -508,12 +508,8 @@
             to = n * 512 + q * 256
             gconv_ref[1 - (k - 2) // 2, :, to : to + 256] = total[:, n * 256 : n * 256 + 256]
 
-    def finish(i, carry):
-        gated_copy(i).wait()
-        e_copy(i).wait()
-        return carry
-
-    lax.fori_loop(0, tiles, finish, 0)
+    pltpu.make_async_copy(X.at[0], gated_hbm, st_g.at[0]).wait()
+    pltpu.make_async_copy(X.at[2], e_hbm, st_e.at[0]).wait()
     wrs_copy.wait()
 
     @pl.when(dp < 7)

time: 95 us -> 95 us (level)
  no operation moved by 1% of the time
where the time goes in v5:
time: 95 us; the launch traced here: 94.8 us
  Pallas kernels  93.4 us (98%)
  between operations  1.44 us (2%)
    pallas_call x1, Pallas kernels, shards(): pl.pallas_call(layer_kernel, out_shape=[out((T, 512), BF16), out((T, 512)...  80.9 us
    pallas_call x1, Pallas kernels, shards(): pl.pallas_call(output_kernel, grid=(T // OUT_TILE,), in_specs=[rows] * 3...  12.5 us

profile of v5, /device:TPU:0, one launch (start us, length us, event | category | flops | bytes accessed | tf_op | source)
XLA Modules:
  0.0 94.8 jit_solution(11414283677413275841)
XLA Ops:
  1.3 80.9 %layer.1 = (bf16[4096,512]{1,0:T(8,128)(2,1)}, bf16[4096,512]{1,0:T(8,128)(2,1)}, bf16[4,2,2,2,16,1024]{5,4,3,2,1,0:T(8,128)(2,1)}, f32[16,1024]{1,0:T(8,128)}, ...) custom-call(s32[1,16]{1,0:T(1,128)} %clip_ref.1, s32[1]{0:T(128)S(6)} %copy.23.dil_ref, ...), custom_call_target="tpu_custom_call" | custom-call | tf_op jit(solution)/shard_map/layer/pallas_call | solution.py:564
  82.2 12.5 %outputs.1 = (bf16[4096,512]{1,0:T(8,128)(2,1)}, bf16[4096,512]{1,0:T(8,128)(2,1)}, f32[4096,512]{1,0:T(8,128)}, f32[2,16,1024]{2,1,0:T(8,128)}, f32[16,512]{1,0...) custom-call(bf16[4096,512]{1,0:T(8,128)(2,1)} %get-tuple-element.28., ...), custom_call_target="tpu_custom_call" | custom-call | tf_op jit(solution)/shard_map/outputs/pallas_call | solution.py:639
